TPU v7x, 128 devices: a whole 4x4x4 slice. The times are simulated.
128 devices in a mesh: section: 4 (over z_hi, core), expert: 32 (over z_lo, y, x).
Axes of the slice: x: 4, y: 4, z: 4 (z_hi: 2, z_lo: 2; z = z_hi * 2 + z_lo), core: 2. Of those that a mesh axis runs over, the one named last changes fastest.
Arguments:
- fwd_tokens: bfloat16 [4, 2560, 3584], P('section', 'expert'), may hold values from -6 to 6
- fwd_routes: int32 [4, 2560, 8], P('section', 'expert'), may hold values from 0 to 31, all different within a row; in each aligned block of 80 rows (0 to 79, 80 to 159, ..., all dimensions but the last counted through in order) at most 21 rows name the same one
- fwd_gates: float32 [4, 2560, 8], P('section', 'expert'), may hold values from 0.05 to 1
- bwd_grads: bfloat16 [4, 2560, 3584], P('section', 'expert'), may hold values from -6 to 6
- bwd_routes: int32 [4, 2560, 8], P('section', 'expert'), may hold values from 0 to 31, all different within a row; in each aligned block of 80 rows (0 to 79, 80 to 159, ..., all dimensions but the last counted through in order) at most 21 rows name the same one
- bwd_gates: float32 [4, 2560, 8], P('section', 'expert'), may hold values from 0.05 to 1
- saved_gate: bfloat16 [4, 2560, 8, 1024], P('section', 'expert'), may hold values from -6 to 6
- saved_up: bfloat16 [4, 2560, 8, 1024], P('section', 'expert'), may hold values from -6 to 6
- w_gate: bfloat16 [4, 32, 3584, 1024], P('section', 'expert'), may hold values from -0.09375 to 0.09375
- w_up: bfloat16 [4, 32, 3584, 1024], P('section', 'expert'), may hold values from -0.09375 to 0.09375
- w_down: bfloat16 [4, 32, 1024, 3584], P('section', 'expert'), may hold values from -0.1875 to 0.1875
Outputs:
- next_inputs: bfloat16 [4, 2560, 3584], P('section', 'expert')
- prev_grads: bfloat16 [4, 2560, 3584], P('section', 'expert')
Inputs may be any that keep to these rules, and one draw needn't show every extreme that they name: `fwd_routes`: each token names 8 different experts. In the rows of one device (80 aligned tokens of one section) no expert is named by more than 21 tokens. `bwd_routes`: as for fwd_routes.
All inputs are finite; a program needn't handle non-finite values.
Results may differ from a plain program's by a relative error of at most 0.0065.
Values may be sent and summed in bfloat16 or wider, within the bound.
A program may use at most 192 MiB of HBM per device.

v0:
```python
import jax
import jax.numpy as jnp
from jax import lax
from jax.sharding import PartitionSpec as P


def from_behind(block, axis, distance):
    devices = range(lax.axis_size(axis))
    route = [((i - distance) % len(devices), i) for i in devices]
    return lax.ppermute(block, axis, route)


def place_rows(routes, groups):
    onehot = (routes[:, :, None] == jnp.arange(groups, dtype=jnp.int32)[None, None, :]).astype(
        jnp.int32
    )
    counts = jnp.sum(onehot, axis=1)
    before = jnp.cumsum(counts, axis=0) - counts
    within = jnp.sum(onehot * before[:, None, :], axis=2)
    return within * groups + routes


def expert_forward(inputs, gate_mat, up_mat, down_mat):
    gate_pre = jnp.dot(inputs, gate_mat, preferred_element_type=jnp.float32)
    up_pre = jnp.dot(inputs, up_mat, preferred_element_type=jnp.float32)
    hidden = (jax.nn.silu(gate_pre) * up_pre).astype(jnp.bfloat16)
    return jnp.dot(hidden, down_mat, preferred_element_type=jnp.float32).astype(jnp.bfloat16)


def expert_backward(scaled, gate_pre, up_pre, gate_mat, up_mat, down_mat):
    numbers = (((1,), (1,)), ((), ()))
    hidden_grad = lax.dot_general(scaled, down_mat, numbers, preferred_element_type=jnp.float32)
    gate_val = gate_pre.astype(jnp.float32)
    up_val = up_pre.astype(jnp.float32)
    sigmoid_a = jax.nn.sigmoid(gate_val)
    gate_grad = (hidden_grad * up_val * sigmoid_a * (1.0 + gate_val * (1.0 - sigmoid_a))).astype(
        jnp.bfloat16
    )
    up_grad = (hidden_grad * gate_val * sigmoid_a).astype(jnp.bfloat16)
    total = lax.dot_general(gate_grad, gate_mat, numbers, preferred_element_type=jnp.float32)
    total = total + lax.dot_general(up_grad, up_mat, numbers, preferred_element_type=jnp.float32)
    return total.astype(jnp.bfloat16)


def body(
    fwd_tokens,
    fwd_routes,
    fwd_gates,
    bwd_grads,
    bwd_routes,
    bwd_gates,
    saved_gate,
    saved_up,
    w_gate,
    w_up,
    w_down,
):
    groups = lax.axis_size("expert")
    inputs = fwd_tokens[0]
    tokens_here = inputs.shape[0]
    width = inputs.shape[1]
    top_count = fwd_routes.shape[2]
    inner = w_gate.shape[3]
    capacity = min(tokens_here, tokens_here * top_count // groups + 1)
    gate_mat = w_gate[0, 0]
    up_mat = w_up[0, 0]
    down_mat = w_down[0, 0]
    fwd_dest = place_rows(fwd_routes[0], groups)
    flat_fwd = fwd_dest.reshape(-1)
    send_fwd = (
        jnp.zeros((capacity * groups, width), jnp.bfloat16)
        .at[flat_fwd]
        .set(jnp.repeat(inputs, top_count, axis=0))
    )
    send_fwd = send_fwd.reshape(capacity, groups, width)
    bwd_dest = place_rows(bwd_routes[0], groups)
    flat_bwd = bwd_dest.reshape(-1)
    scaled = (bwd_gates[0][:, :, None] * bwd_grads[0][:, None, :].astype(jnp.float32)).astype(
        jnp.bfloat16
    )
    send_grad = (
        jnp.zeros((capacity * groups, width), jnp.bfloat16)
        .at[flat_bwd]
        .set(scaled.reshape(-1, width))
    )
    send_gate = (
        jnp.zeros((capacity * groups, inner), jnp.bfloat16)
        .at[flat_bwd]
        .set(saved_gate[0].reshape(-1, inner))
    )
    send_up = (
        jnp.zeros((capacity * groups, inner), jnp.bfloat16)
        .at[flat_bwd]
        .set(saved_up[0].reshape(-1, inner))
    )
    send_grad = send_grad.reshape(capacity, groups, width)
    send_gate = send_gate.reshape(capacity, groups, inner)
    send_up = send_up.reshape(capacity, groups, inner)
    arrived = lax.all_to_all(send_fwd, "expert", split_axis=1, concat_axis=1, tiled=True)
    slots_here = arrived.shape[0]
    fwd_rows = expert_forward(arrived.reshape(-1, width), gate_mat, up_mat, down_mat)
    back_fwd = lax.all_to_all(
        fwd_rows.reshape(slots_here, groups, width),
        "expert",
        split_axis=1,
        concat_axis=1,
        tiled=True,
    )
    grad_rows = lax.all_to_all(send_grad, "expert", split_axis=1, concat_axis=1, tiled=True)
    gate_rows = lax.all_to_all(send_gate, "expert", split_axis=1, concat_axis=1, tiled=True)
    up_rows = lax.all_to_all(send_up, "expert", split_axis=1, concat_axis=1, tiled=True)
    slots_here = grad_rows.shape[0]
    bwd_rows = expert_backward(
        grad_rows.reshape(-1, width),
        gate_rows.reshape(-1, inner),
        up_rows.reshape(-1, inner),
        gate_mat,
        up_mat,
        down_mat,
    )
    back_bwd = lax.all_to_all(
        bwd_rows.reshape(slots_here, groups, width),
        "expert",
        split_axis=1,
        concat_axis=1,
        tiled=True,
    )
    picked_fwd = back_fwd.reshape(capacity * groups, width)[fwd_dest].astype(jnp.float32)
    fwd_out = jnp.sum(fwd_gates[0][:, :, None] * picked_fwd, axis=1).astype(jnp.bfloat16)
    picked_bwd = back_bwd.reshape(capacity * groups, width)[bwd_dest].astype(jnp.float32)
    bwd_out = jnp.sum(picked_bwd, axis=1).astype(jnp.bfloat16)
    next_inputs = from_behind(fwd_out, "section", 1)
    prev_grads = from_behind(bwd_out, "section", -1)
    return (next_inputs[None], prev_grads[None])


def solution(mesh):
    return jax.shard_map(
        body,
        mesh=mesh,
        in_specs=(
            P("section", "expert", None),
            P("section", "expert", None),
            P("section", "expert", None),
            P("section", "expert", None),
            P("section", "expert", None),
            P("section", "expert", None),
            P("section", "expert", None, None),
            P("section", "expert", None, None),
            P("section", "expert", None, None),
            P("section", "expert", None, None),
            P("section", "expert", None, None),
        ),
        out_specs=(P("section", "expert", None), P("section", "expert", None)),
        check_vma=False,
    )
```

profile of v0, /device:TPU:10, one launch (start us, length us, event | category | flops | bytes accessed | tf_op | source)
XLA Modules:
  0.0 428.4 jit_solution(7810578604573362577)
XLA Ops:
  0.6 0.9 copy.105
  1.5 0.7 convert_reduce_fusion
  2.2 0.1 copy.101
  2.3 0.1 reduce_window_sum.18
  2.5 0.7 select_reduce_fusion
  3.3 0.1 copy.104
  3.3 0.1 mul.130
  3.4 0.1 squeeze.28
  3.6 6.4 %scatter_custom_fusion.3 = bf16[672,1024]{1,0:T(8,128)(2,1)S(1)} fusion(s32[640]{0:T(1024)S(1)} %fusion.53, bf16[1,80,8,1024]{3,2,1,0:T(8,128)(2,1)S(1)} %copy-done, bf16[]{:T(256)} %constant.7.clone.1), kind=kCustom, calls=%fused_computation.50 | custom fusion | bytes 2686978 | tf_op jit(solution)/shard_map/scatter | solution.py:89
  10.0 1.9 copy.111
  11.9 8.9 %all-to-all-start.4 = ((bf16[21,32,1024]{2,0,1:T(8,128)(2,1)}), bf16[21,32,1024]{2,0,1:T(8,128)(2,1)S(1)}, u32[]{:S(2)}, u32[]{:S(2)}) async-start(bf16[21,32,1024]{2,0,1:T(8,128)(2,1)} %copy.111), calls=%async_computation.4 | async-start | bytes 3145728 | tf_op jit(solution)/shard_map/all_to_all | solution.py:110
  20.9 7.2 %scatter_custom_fusion.2 = bf16[672,1024]{1,0:T(8,128)(2,1)} fusion(s32[640]{0:T(1024)S(1)} %fusion.53, bf16[1,80,8,1024]{3,2,1,0:T(8,128)(2,1)S(1)} %copy-done.4, bf16[]{:T(256)} %constant.7.clone.1), kind=kCustom, calls=%fused_computation.52 | custom fusion | bytes 2686978 | tf_op jit(solution)/shard_map/scatter | solution.py:94
  28.1 3.3 copy.109
  31.4 9.3 %all-to-all-done.4 = bf16[21,32,1024]{2,0,1:T(8,128)(2,1)S(1)} async-done(((bf16[21,32,1024]{2,0,1:T(8,128)(2,1)}), bf16[21,32,1024]{2,0,1:T(8,128)(2,1)S(1)}, u32[]{:S(2)}, u32[]{:S(2)}) %all-to-all-start.4) | async-done | bytes 1376288 | tf_op jit(solution)/shard_map/all_to_all | solution.py:110
  40.7 7.8 %all-to-all-start.3 = ((bf16[21,32,1024]{2,0,1:T(8,128)(2,1)}), bf16[21,32,1024]{2,0,1:T(8,128)(2,1)}, u32[]{:S(2)}, u32[]{:S(2)}) async-start(bf16[21,32,1024]{2,0,1:T(8,128)(2,1)} %copy.109), calls=%async_computation.3 | async-start | bytes 3145728 | tf_op jit(solution)/shard_map/all_to_all | solution.py:111
  48.5 0.1 copy.106
  48.6 0.1 mul.131
  48.7 0.1 bitcast_convert_fusion
  48.8 16.4 %scatter_custom_fusion.1 = bf16[672,3584]{1,0:T(8,128)(2,1)} fusion(s32[640]{0:T(1024)S(1)} %fusion.53, f32[80,3584]{1,0:T(8,128)S(1)} %bitcast_convert_fusion, f32[640]{0:T(1024)S(1)} %mul.131, bf16[]{:T(256)} %constant.7.clone.1), kind=kCustom, calls=%fused_computation.24 | custom fusion | flops 4587520 | bytes 5967874 | tf_op jit(solution)/shard_map/scatter | solution.py:84
  65.2 7.4 %copy.107 = bf16[21,32,3584]{2,0,1:T(8,128)(2,1)} copy(bf16[21,32,3584]{2,1,0:T(8,128)(2,1)} %bitcast.86) | data formatting | bytes 9633792 | tf_op jit(solution)/shard_map/reshape | solution.py:96
  72.6 8.8 %all-to-all-start.2 = ((bf16[21,32,3584]{2,0,1:T(8,128)(2,1)}), bf16[21,32,3584]{2,0,1:T(8,128)(2,1)}, u32[]{:S(2)}, u32[]{:S(2)}) async-start(bf16[21,32,3584]{2,0,1:T(8,128)(2,1)} %copy.107), calls=%async_computation.2 | async-start | bytes 11010048 | tf_op jit(solution)/shard_map/all_to_all | solution.py:109
  81.4 0.1 copy.95
  81.5 0.1 copy.91
  81.6 0.1 reduce_window_sum.17
  81.8 0.1 copy.94
  81.9 0.1 mul.122
  82.0 0.1 squeeze.22
  82.1 13.3 %scatter_custom_fusion = bf16[672,3584]{1,0:T(8,128)(2,1)} fusion(s32[640]{0:T(1024)S(1)} %fusion.52, bf16[]{:T(256)} %constant.7.clone.1, bf16[80,3584]{1,0:T(8,128)(2,1)S(1)} %bitcast.100), kind=kCustom, calls=%fused_computation.26 | custom fusion | bytes 5390338 | tf_op jit(solution)/shard_map/scatter | solution.py:73
  95.4 7.4 %copy.96 = bf16[21,32,3584]{2,0,1:T(8,128)(2,1)} copy(bf16[21,32,3584]{2,1,0:T(8,128)(2,1)} %bitcast.87) | data formatting | bytes 9633792 | tf_op jit(solution)/shard_map/reshape | solution.py:75
  102.9 1.9 copy.112
  104.8 2.2 copy.110
  107.0 46.4 %all-to-all-done.2 = bf16[21,32,3584]{2,0,1:T(8,128)(2,1)} async-done(((bf16[21,32,3584]{2,0,1:T(8,128)(2,1)}), bf16[21,32,3584]{2,0,1:T(8,128)(2,1)}, u32[]{:S(2)}, u32[]{:S(2)}) %all-to-all-start.2) | async-done | bytes 4816928 | tf_op jit(solution)/shard_map/all_to_all | solution.py:109
  153.4 4.9 %all-to-all-start = ((bf16[21,32,3584]{2,0,1:T(8,128)(2,1)}), bf16[21,32,3584]{2,0,1:T(8,128)(2,1)}, u32[]{:S(2)}, u32[]{:S(2)}) async-start(bf16[21,32,3584]{2,0,1:T(8,128)(2,1)} %copy.96), calls=%async_computation | async-start | bytes 11010048 | tf_op jit(solution)/shard_map/all_to_all | solution.py:99
  158.3 4.2 copy.108
  162.5 7.6 %fusion.2 = f32[672,1024]{1,0:T(8,128)S(1)} fusion(bf16[672,3584]{1,0:T(8,128)(2,1)S(1)} %bitcast.94, bf16[1,1,1024,3584]{3,2,1,0:T(8,128)(2,1)} %param.21), kind=kOutput, calls=%fused_computation.11 | convolution fusion | flops 4932501504 | bytes 14909440 | tf_op jit(solution)/shard_map/dot_general | solution.py:32
  170.2 8.5 %fusion.6 = f32[672,3584]{1,0:T(8,128)} fusion(bf16[1,1,3584,1024]{3,2,1,0:T(8,128)(2,1)S(1)} %bitcast.107, f32[672,1024]{1,0:T(8,128)S(1)} %fusion.2, bf16[672,1024]{1,0:T(8,128)(2,1)S(1)} %bitcast.95), kind=kOutput, calls=%fused_computation.15 | convolution fusion | flops 4937318400 | bytes 21102592 | tf_op jit(solution)/shard_map/dot_general | solution.py:41
  178.7 10.7 %add_convert_fusion = bf16[672,3584]{1,0:T(8,128)(2,1)S(1)} fusion(f32[672,3584]{1,0:T(8,128)} %fusion.6, bf16[1,1,3584,1024]{3,2,1,0:T(8,128)(2,1)} %param.19, bf16[672,1024]{1,0:T(8,128)(2,1)S(1)} %bitcast.96, f32[672,1024]{1,0:T(8,128)S(1)} %fusion.2, bf16[672,1024]{1,0:T(8,128)(2,1)S(1)} %bitcast.97), kind=kOutput, calls=%fused_computation.6 | convolution fusion | flops 4945575936 | bytes 27295744 | tf_op jit(solution)/shard_map/dot_general | solution.py:40
  189.4 5.1 %copy.113 = bf16[21,32,3584]{2,0,1:T(8,128)(2,1)} copy(bf16[21,32,3584]{2,1,0:T(8,128)(2,1)S(1)} %bitcast.90) | data formatting | bytes 9633792 | tf_op jit(solution)/shard_map/reshape | solution.py:122
  194.5 40.0 %all-to-all-done = bf16[21,32,3584]{2,0,1:T(8,128)(2,1)} async-done(((bf16[21,32,3584]{2,0,1:T(8,128)(2,1)}), bf16[21,32,3584]{2,0,1:T(8,128)(2,1)}, u32[]{:S(2)}, u32[]{:S(2)}) %all-to-all-start) | async-done | bytes 4816928 | tf_op jit(solution)/shard_map/all_to_all | solution.py:99
  234.5 8.1 %all-to-all-start.5 = ((bf16[21,32,3584]{2,0,1:T(8,128)(2,1)}), bf16[21,32,3584]{2,0,1:T(8,128)(2,1)}, u32[]{:S(2)}, u32[]{:S(2)}) async-start(bf16[21,32,3584]{2,0,1:T(8,128)(2,1)} %copy.113), calls=%async_computation.5 | async-start | bytes 11010048 | tf_op jit(solution)/shard_map/all_to_all | solution.py:121
  242.6 4.0 copy.97
  246.6 2.2 copy-done.2
  248.9 8.5 %fusion.8 = f32[672,1024]{1,0:T(8,128)} fusion(bf16[672,3584]{1,0:T(8,128)(2,1)S(1)} %bitcast.91, bf16[1,1,3584,1024]{3,2,1,0:T(8,128)(2,1)} %param.20), kind=kOutput, calls=%fused_computation.17 | convolution fusion | flops 4932501504 | bytes 14909440 | tf_op jit(solution)/shard_map/dot_general | solution.py:25
  257.4 18.1 %fusion.14 = bf16[672,3584]{1,0:T(8,128)(2,1)} fusion(bf16[1,1,1024,3584]{3,2,1,0:T(8,128)(2,1)} %param.21, f32[672,1024]{1,0:T(8,128)} %fusion.8, bf16[672,3584]{1,0:T(8,128)(2,1)} %bitcast.92, bf16[1,1,3584,1024]{3,2,1,0:T(8,128)(2,1)} %param.19), kind=kOutput, calls=%fused_computation.23 | convolution fusion | flops 9871540224 | bytes 27066368 | tf_op jit(solution)/shard_map/dot_general | solution.py:27
  275.5 7.4 %copy.98 = bf16[21,32,3584]{2,0,1:T(8,128)(2,1)} copy(bf16[21,32,3584]{2,1,0:T(8,128)(2,1)} %bitcast.93) | data formatting | bytes 9633792 | tf_op jit(solution)/shard_map/reshape | solution.py:103
  282.9 29.0 %all-to-all-done.5 = bf16[21,32,3584]{2,0,1:T(8,128)(2,1)} async-done(((bf16[21,32,3584]{2,0,1:T(8,128)(2,1)}), bf16[21,32,3584]{2,0,1:T(8,128)(2,1)}, u32[]{:S(2)}, u32[]{:S(2)}) %all-to-all-start.5) | async-done | bytes 4816928 | tf_op jit(solution)/shard_map/all_to_all | solution.py:121
  311.9 6.2 %all-to-all-start.1 = ((bf16[21,32,3584]{2,0,1:T(8,128)(2,1)}), bf16[21,32,3584]{2,0,1:T(8,128)(2,1)}, u32[]{:S(2)}, u32[]{:S(2)}) async-start(bf16[21,32,3584]{2,0,1:T(8,128)(2,1)} %copy.98), calls=%async_computation.1 | async-start | bytes 11010048 | tf_op jit(solution)/shard_map/all_to_all | solution.py:102
  318.1 0.1 copy.115
  318.2 0.1 reshape.226
  318.3 0.1 copy.100
  318.4 0.1 reshape.218
  318.5 0.1 copy.90
  318.6 6.2 %copy.114 = bf16[21,32,3584]{2,1,0:T(8,128)(2,1)} copy(bf16[21,32,3584]{2,0,1:T(8,128)(2,1)} %all-to-all-done.5) | data formatting | bytes 9633792 | tf_op jit(solution)/shard_map/all_to_all | solution.py:121
  324.8 13.6 %gather_fusion.1 = bf16[640,3584]{1,0:T(8,128)(2,1)} fusion(bf16[672,3584]{1,0:T(8,128)(2,1)} %bitcast.84, s32[1024]{0:T(1024)S(1)} %pad_clamp_fusion), kind=kCustom, calls=%fused_computation.1 | custom fusion | bytes 9177600 | tf_op jit(solution)/shard_map/gather | solution.py:130
  338.4 5.4 %bitcast_reduce_fusion = bf16[80,3584]{1,0:T(8,128)(2,1)S(1)} fusion(bf16[640,3584]{1,0:T(8,128)(2,1)} %gather_fusion.1), kind=kLoop, calls=%fused_computation.25 | loop fusion | flops 2007040 | bytes 5160960 | tf_op jit(solution)/shard_map/reduce_sum | solution.py:131
  343.8 2.2 collective-permute-start.1
  345.9 43.7 %all-to-all-done.1 = bf16[21,32,3584]{2,0,1:T(8,128)(2,1)} async-done(((bf16[21,32,3584]{2,0,1:T(8,128)(2,1)}), bf16[21,32,3584]{2,0,1:T(8,128)(2,1)}, u32[]{:S(2)}, u32[]{:S(2)}) %all-to-all-start.1) | async-done | bytes 4816928 | tf_op jit(solution)/shard_map/all_to_all | solution.py:102
  389.7 6.2 %copy.99 = bf16[21,32,3584]{2,1,0:T(8,128)(2,1)} copy(bf16[21,32,3584]{2,0,1:T(8,128)(2,1)} %all-to-all-done.1) | data formatting | bytes 9633792 | tf_op jit(solution)/shard_map/all_to_all | solution.py:102
  395.9 13.8 %gather_fusion = bf16[640,3584]{1,0:T(8,128)(2,1)} fusion(bf16[672,3584]{1,0:T(8,128)(2,1)} %bitcast.85, s32[1024]{0:T(1024)S(1)} %pad_clamp_fusion.1), kind=kCustom, calls=%fused_computation | custom fusion | bytes 9177600 | tf_op jit(solution)/shard_map/gather | solution.py:128
  409.7 6.2 %fusion = bf16[80,3584]{1,0:T(8,128)(2,1)S(1)} fusion(bf16[640,3584]{1,0:T(8,128)(2,1)} %gather_fusion, f32[80,8]{1,0:T(8,128)S(1)} %copy.90), kind=kLoop, calls=%fused_computation.8 | loop fusion | flops 6594560 | bytes 5163520 | tf_op jit(solution)/shard_map/reduce_sum | solution.py:129
  415.8 0.1 collective-permute-start
  415.9 10.6 %collective-permute-done = bf16[80,3584]{1,0:T(8,128)(2,1)S(1)} collective-permute-done((bf16[80,3584]{1,0:T(8,128)(2,1)S(1)}, bf16[80,3584]{1,0:T(8,128)(2,1)S(1)}, u32[]{:S(2)}, u32[]{:S(2)}) %collective-permute-start) | collective-permute-done | bytes 573472 | tf_op jit(solution)/shard_map/ppermute | solution.py:10
  426.6 0.8 copy.118
  427.4 0.8 copy.119
  (42 shorter events, 0.3 us)
Async XLA Ops:
  0.6 2.9 copy-start
  10.0 10.8 %copy-start.4 = (bf16[1,80,8,1024]{3,2,1,0:T(8,128)(2,1)S(1)}, bf16[1,80,8,1024]{3,2,1,0:T(8,128)(2,1)}, u32[]{:S(2)}) copy-start(bf16[1,80,8,1024]{3,2,1,0:T(8,128)(2,1)} %param.18) | copy-start | bytes 3932164
  11.9 28.7 %all-to-all-start.4 = ((bf16[21,32,1024]{2,0,1:T(8,128)(2,1)}), bf16[21,32,1024]{2,0,1:T(8,128)(2,1)S(1)}, u32[]{:S(2)}, u32[]{:S(2)}) async-start(bf16[21,32,1024]{2,0,1:T(8,128)(2,1)} %copy.111), calls=%async_computation.4 | async-start | bytes 3145728 | tf_op jit(solution)/shard_map/all_to_all | solution.py:110
  20.8 27.7 %copy-start.9 = (f32[1,80,8]{1,2,0:T(8,128)S(1)}, f32[1,80,8]{1,2,0:T(8,128)}, u32[]{:S(2)}) copy-start(f32[1,80,8]{1,2,0:T(8,128)} %param.16) | copy-start | bytes 7684
  20.8 27.9 %copy-start.5 = (bf16[1,80,3584]{2,1,0:T(8,128)(2,1)S(1)}, bf16[1,80,3584]{2,1,0:T(8,128)(2,1)}, u32[]{:S(2)}) copy-start(bf16[1,80,3584]{2,1,0:T(8,128)(2,1)} %param.14) | copy-start | bytes 1720324
  40.7 31.9 %all-to-all-start.3 = ((bf16[21,32,1024]{2,0,1:T(8,128)(2,1)}), bf16[21,32,1024]{2,0,1:T(8,128)(2,1)}, u32[]{:S(2)}, u32[]{:S(2)}) async-start(bf16[21,32,1024]{2,0,1:T(8,128)(2,1)} %copy.109), calls=%async_computation.3 | async-start | bytes 3145728 | tf_op jit(solution)/shard_map/all_to_all | solution.py:111
  72.6 8.8 %copy-start.8 = (s32[1,80,8]{1,2,0:T(8,128)S(1)}, s32[1,80,8]{1,2,0:T(8,128)}, u32[]{:S(2)}) copy-start(s32[1,80,8]{1,2,0:T(8,128)} %param.12) | copy-start | bytes 7684
  72.6 9.5 %copy-start.6 = (bf16[1,80,3584]{2,1,0:T(8,128)(2,1)S(1)}, bf16[1,80,3584]{2,1,0:T(8,128)(2,1)}, u32[]{:S(2)}) copy-start(bf16[1,80,3584]{2,1,0:T(8,128)(2,1)} %param.11) | copy-start | bytes 1720324
  72.6 80.8 %all-to-all-start.2 = ((bf16[21,32,3584]{2,0,1:T(8,128)(2,1)}), bf16[21,32,3584]{2,0,1:T(8,128)(2,1)}, u32[]{:S(2)}, u32[]{:S(2)}) async-start(bf16[21,32,3584]{2,0,1:T(8,128)(2,1)} %copy.107), calls=%async_computation.2 | async-start | bytes 11010048 | tf_op jit(solution)/shard_map/all_to_all | solution.py:109
  153.4 81.1 %all-to-all-start = ((bf16[21,32,3584]{2,0,1:T(8,128)(2,1)}), bf16[21,32,3584]{2,0,1:T(8,128)(2,1)}, u32[]{:S(2)}, u32[]{:S(2)}) async-start(bf16[21,32,3584]{2,0,1:T(8,128)(2,1)} %copy.96), calls=%async_computation | async-start | bytes 11010048 | tf_op jit(solution)/shard_map/all_to_all | solution.py:99
  158.3 11.8 %slice-start = ((s8[7340032]{0:T(1024)(128)(4,1)}), s8[4194304]{0:T(1024)(128)(4,1)S(1)}, s32[]{:S(2)}) async-start(s8[7340032]{0:T(1024)(128)(4,1)} %bitcast.106), calls=%async_computation.6 | async-start | bytes 8388608
  162.5 7.6 %copy-start.3 = (bf16[21,32,1024]{2,1,0:T(8,128)(2,1)S(1)}, bf16[21,32,1024]{2,1,0:T(8,128)(2,1)}, u32[]{:S(2)}) copy-start(bf16[21,32,1024]{2,1,0:T(8,128)(2,1)} %copy.112) | copy-start | bytes 4128772
  162.5 7.6 %slice-start.1 = ((s8[7340032]{0:T(1024)(128)(4,1)}), s8[3145728]{0:T(1024)(128)(4,1)S(1)}, s32[]{:S(2)}) async-start(s8[7340032]{0:T(1024)(128)(4,1)} %bitcast.106), calls=%async_computation.7 | async-start | bytes 6291456
  234.5 77.4 %all-to-all-start.5 = ((bf16[21,32,3584]{2,0,1:T(8,128)(2,1)}), bf16[21,32,3584]{2,0,1:T(8,128)(2,1)}, u32[]{:S(2)}, u32[]{:S(2)}) async-start(bf16[21,32,3584]{2,0,1:T(8,128)(2,1)} %copy.113), calls=%async_computation.5 | async-start | bytes 11010048 | tf_op jit(solution)/shard_map/all_to_all | solution.py:121
  246.6 2.2 copy-start.2
  282.9 35.2 %copy-start.7 = (s32[1,80,8]{1,2,0:T(8,128)S(1)}, s32[1,80,8]{1,2,0:T(8,128)}, u32[]{:S(2)}) copy-start(s32[1,80,8]{1,2,0:T(8,128)} %param.15) | copy-start | bytes 7684
  282.9 35.6 %copy-start.10 = (f32[1,80,8]{1,2,0:T(8,128)S(1)}, f32[1,80,8]{1,2,0:T(8,128)}, u32[]{:S(2)}) copy-start(f32[1,80,8]{1,2,0:T(8,128)} %param.13) | copy-start | bytes 7684
  311.9 77.8 %all-to-all-start.1 = ((bf16[21,32,3584]{2,0,1:T(8,128)(2,1)}), bf16[21,32,3584]{2,0,1:T(8,128)(2,1)}, u32[]{:S(2)}, u32[]{:S(2)}) async-start(bf16[21,32,3584]{2,0,1:T(8,128)(2,1)} %copy.98), calls=%async_computation.1 | async-start | bytes 11010048 | tf_op jit(solution)/shard_map/all_to_all | solution.py:102
  343.8 72.1 %collective-permute-start.1 = (bf16[80,3584]{1,0:T(8,128)(2,1)S(1)}, bf16[80,3584]{1,0:T(8,128)(2,1)S(1)}, u32[]{:S(2)}, u32[]{:S(2)}) collective-permute-start(bf16[80,3584]{1,0:T(8,128)(2,1)S(1)} %bitcast_reduce_fusion), channel_id=1, source_target_pairs={{32,0},{64,32},{96,64},{0,96},{33,1},{65,33},{97,65},{1,97},{34,2}... | collective-permute-start | bytes 1720328 | tf_op jit(solution)/shard_map/ppermute | solution.py:10
  395.9 32.3 %copy-start.1 = (bf16[1,80,8,1024]{3,2,1,0:T(8,128)(2,1)S(1)}, bf16[1,80,8,1024]{3,2,1,0:T(8,128)(2,1)}, u32[]{:S(2)}) copy-start(bf16[1,80,8,1024]{3,2,1,0:T(8,128)(2,1)} %param.17) | copy-start | bytes 3932164
  415.8 10.7 %collective-permute-start = (bf16[80,3584]{1,0:T(8,128)(2,1)S(1)}, bf16[80,3584]{1,0:T(8,128)(2,1)S(1)}, u32[]{:S(2)}, u32[]{:S(2)}) collective-permute-start(bf16[80,3584]{1,0:T(8,128)(2,1)S(1)} %fusion), channel_id=1, source_target_pairs={{96,0},{0,32},{32,64},{64,96},{97,1},{1,33},{33,65},{65,97},{98,2}... | collective-permute-start | bytes 1720328 | tf_op jit(solution)/shard_map/ppermute | solution.py:10
where the time goes:
time: 437 us; the launch traced here: 428 us
  waiting for transfers between devices  179 us (41%)
  local copies, waits for them, and re-layouts  118 us (27%)
  matrix products  53.4 us (12%)
  starting transfers between devices  46.8 us (11%)
  other arithmetic  29.8 us (7%)
    all_to_all x1, waiting for transfers between devices, body(): lax.all_to_all(send_grad, 'expert', split_axis=1, concat_axis=1, tiled=True)  46.4 us
    all_to_all x1, waiting for transfers between devices, body(): lax.all_to_all(fwd_rows.reshape(slots_here, groups, width), 'expert', spl...  43.7 us
    all_to_all x1, waiting for transfers between devices, body(): lax.all_to_all(send_fwd, 'expert', split_axis=1, concat_axis=1, tiled=True)  40 us
    all_to_all x1, waiting for transfers between devices, body(): lax.all_to_all(bwd_rows.reshape(slots_here, groups, width), 'expert', spl...  29 us
    dot_general x1, matrix products, expert_forward(): jnp.dot(hidden, down_mat, preferred_element_type=jnp.float32)  18.1 us
    scatter x1, other arithmetic, body(): send_grad = jnp.zeros((capacity * groups, width), jnp.bfloat16).at[flat_b...  16.4 us
    gather x1, local copies, waits for them, and re-layouts, body(): back_fwd.reshape(capacity * groups, width)[fwd_dest].astype(jnp.float32)  13.8 us
    gather x1, local copies, waits for them, and re-layouts, body(): back_bwd.reshape(capacity * groups, width)[bwd_dest].astype(jnp.float32)  13.6 us
  transfers between devices with their start and end apart: 8, of which 6 were waited for; matrix products, arithmetic and copies ran while one was open for 43% of the time, Pallas kernels for 0%

commit v1 on v0

v1 whole, which is shorter than its diff:
```python
import functools

import jax
import jax.numpy as jnp
import numpy as np
from jax import lax
from jax.experimental import pallas as pl
from jax.experimental.pallas import tpu as pltpu
from jax.sharding import PartitionSpec as P

MESH = pl.DeviceIdType.MESH
F32 = jnp.float32
BF16 = jnp.bfloat16

RING = 4
CAP = 21
TOK = 80
GROUP = RING * CAP
EXTRA = GROUP - TOK
MAIN = RING * TOK
ROWS = RING * GROUP
TAIL = ROWS - MAIN
LANES = 128
N_SEMS = 132
N_LOCAL = 24


def row_of(block, place):
    return block * TOK + place if place < TOK else MAIN + block * EXTRA + place - TOK


def swap_matrix():
    m = np.zeros((ROWS, ROWS), np.float32)
    for q in range(RING):
        for t in range(RING):
            for i in range(CAP):
                m[row_of(t, q * CAP + i), row_of(q, t * CAP + i)] = 1
    return m


def fold_matrix():
    m = np.zeros((4 * TAIL, 4 * TAIL), np.float32)
    for a in range(4):
        for b in range(4):
            for j in range(4):
                m[b * 16 + a * 4 + j, a * 16 + b * 4 + j] = 1
    return m


def dot(a, b):
    return jnp.dot(a, b, preferred_element_type=F32)


def dot_t(a, b):
    return lax.dot_general(a, b, (((1,), (1,)), ((), ())), preferred_element_type=F32)


def aligned(i, size):
    return pl.ds(pl.multiple_of(i * size, size), size)


def kernel(
    tok_hbm,
    grd_hbm,
    sg_hbm,
    su_hbm,
    wg_hbm,
    wu_hbm,
    wd_hbm,
    meta,
    spos,
    fold,
    swap,
    out_f,
    out_b,
    g_fo, g_fp, g_bo, g_bp,
    pk_fo, pk_fp, pk_bo, pk_bp,
    x_f, x_b,
    es, er, ys, yr,
    ra, rb, rc, rd, zr,
    mo, mz, mp,
    spk_o, spk_p, sg_o, sg_p, sz, sx,
    spe, sge, sze, s2e, sxe,
    hb, oh, wa, wd_t,
    send, recv, local, wsem,
):
    e = lax.axis_index("expert")
    sec = lax.axis_index("section")
    n_sec = lax.axis_size("section")
    z, y, x = e // 16, lax.rem(e // 4, 4), lax.rem(e, 4)
    me = {"y": y, "x": x}
    width = tok_hbm.shape[1]
    inner = wg_hbm.shape[1]
    half = width // 2
    F, B, O, Q = 0, 1, 0, 1
    G = ((g_fo, g_fp), (g_bo, g_bp))
    PK = ((pk_fo, pk_fp), (pk_bo, pk_bp))
    X = (x_f, x_b)
    AG_AXIS = ("y", "x")
    UNI_AXIS = ("x", "y")

    def at(axis, c):
        if axis == "y":
            return (sec, z * 16 + c * 4 + x)
        return (sec, z * 16 + y * 4 + c)

    def peer(axis, k):
        return at(axis, lax.rem(me[axis] + k, RING))

    partner = (sec, (1 - z) * 16 + y * 4 + x)
    next_sec = (lax.rem(sec + 1, n_sec), e)
    prev_sec = (lax.rem(sec + n_sec - 1, n_sec), e)

    used = [0, 0]

    def remote(src, dst, device):
        i = used[0]
        used[0] += 1
        cp = pltpu.make_async_remote_copy(
            src_ref=src, dst_ref=dst, send_sem=send.at[i], recv_sem=recv.at[i],
            device_id=device, device_id_type=MESH,
        )
        cp.start()
        return cp

    def here(src, dst):
        i = used[1]
        used[1] += 1
        cp = pltpu.make_async_copy(src, dst, local.at[i])
        cp.start()
        return cp

    def wait_recv(cps):
        for cp in cps:
            cp.wait_recv()

    def wait_send(cps):
        for cp in cps:
            cp.wait_send()

    def wa_pair(j, slot):
        cols = pl.ds(pl.multiple_of(j * LANES, LANES), LANES)
        return (
            pltpu.make_async_copy(wg_hbm.at[:, cols], wa.at[slot, :, 0:LANES], wsem.at[0, slot]),
            pltpu.make_async_copy(wu_hbm.at[:, cols], wa.at[slot, :, LANES : 2 * LANES], wsem.at[1, slot]),
        )

    def wa_down(j, slot):
        cols = pl.ds(pl.multiple_of(j * 256, 256), 256)
        return (pltpu.make_async_copy(wd_hbm.at[:, cols], wa.at[slot, 0:inner, :], wsem.at[0, slot]),)

    def wd_rows(j, slot):
        rows = aligned(j, 256)
        return (pltpu.make_async_copy(wd_hbm.at[rows, :], wd_t.at[slot], wsem.at[2, slot]),)

    def wd_pair(j, slot):
        rows = aligned(j, 256)
        return (
            pltpu.make_async_copy(wg_hbm.at[rows, :], wd_t.at[slot, :, 0:inner], wsem.at[2, slot]),
            pltpu.make_async_copy(wu_hbm.at[rows, :], wd_t.at[slot, :, inner : 2 * inner], wsem.at[3, slot]),
        )

    def begin(tiles):
        for cp in tiles(0, 0):
            cp.start()

    def stream(n, tiles, work):
        def step(j, carry):
            slot = lax.rem(j, 2)

            @pl.when(j + 1 < n)
            def _():
                for cp in tiles(j + 1, 1 - slot):
                    cp.start()

            for cp in tiles(j, slot):
                cp.wait()
            work(j, slot)
            return carry

        lax.fori_loop(0, n, step, 0)

    def fold_out(src, row0, dst):
        w4 = src.shape[1] // 4
        a = jnp.concatenate([src[row0 : row0 + TAIL, c * w4 : (c + 1) * w4] for c in range(4)], axis=0)
        dst[...] = dot(fold[...], a).astype(BF16)

    def fold_in(src, dst, row0):
        w4 = dst.shape[1] // 4
        a = dot(fold[...], src[...]).astype(BF16)
        for c in range(4):
            dst[row0 : row0 + TAIL, c * w4 : (c + 1) * w4] = a[c * TAIL : (c + 1) * TAIL, :]

    def exchange(axis, src, src_off, src_extra, dst, dst_off, dst_extra):
        m = me[axis]
        cps = []
        for k in (2, 1, 3):
            c = lax.rem(m + k, RING)
            cps.append(remote(
                src.at[pl.ds(pl.multiple_of(src_off + c * TOK, 16), TOK), :],
                dst.at[pl.ds(pl.multiple_of(dst_off + m * TOK, 16), TOK), :],
                at(axis, c)))
            cps.append(remote(src_extra.at[aligned(c, TAIL), :], dst_extra.at[aligned(m, TAIL), :], at(axis, c)))
        own = here(
            src.at[pl.ds(pl.multiple_of(src_off + m * TOK, 16), TOK), :],
            dst.at[pl.ds(pl.multiple_of(dst_off + m * TOK, 16), TOK), :])
        dst_extra[aligned(m, TAIL), :] = src_extra[aligned(m, TAIL), :]
        return cps, own

    def slot_of(ref, c, cols=None):
        rows = pl.ds(pl.multiple_of(c * TOK, 16), TOK)
        return ref.at[rows, :] if cols is None else ref.at[rows, cols]

    LO, HI = pl.ds(0, half), pl.ds(half, half)

    def gather_begin(axis, ref):
        m = me[axis]
        return [remote(slot_of(ref, m), slot_of(ref, m), peer(axis, 1)),
                remote(slot_of(ref, m), slot_of(ref, m), peer(axis, 3))]

    def gather_relay(axis, ref, first):
        m = me[axis]
        before, after = lax.rem(m + 3, RING), lax.rem(m + 1, RING)
        first[0].wait_recv()
        a = remote(slot_of(ref, before, LO), slot_of(ref, before, LO), peer(axis, 1))
        first[1].wait_recv()
        b = remote(slot_of(ref, after, HI), slot_of(ref, after, HI), peer(axis, 3))
        return [a, b]

    def pack(f, g):
        wide = lax.broadcasted_iota(jnp.int32, (TOK, LANES), 0).astype(F32)
        tail = lax.broadcasted_iota(jnp.int32, (TAIL, LANES), 0)
        tail_place = (TOK + lax.rem(tail, EXTRA)).astype(F32)
        tail_block = tail // EXTRA
        metas = (mo, mp)[g]
        for q in range(RING):
            s = metas[f, q].astype(F32)
            s = jnp.where(s >= 0, s + q * CAP, -1.0)
            cols = slice(q * LANES, (q + 1) * LANES)
            chosen = jnp.zeros((TAIL, LANES), F32)
            for t in range(RING):
                row = s[t : t + 1, :]
                oh[t * TOK : (t + 1) * TOK, cols] = jnp.where(wide == row, 1.0, 0.0).astype(BF16)
                chosen = jnp.where(tail_block == t, row, chosen)
            oh[MAIN:ROWS, cols] = jnp.where(chosen == tail_place, 1.0, 0.0).astype(BF16)

        def cols_step(j, carry):
            cols = aligned(j, 512)
            acc = dot(oh[:, 0:TOK], G[f][g][0:TOK, cols])
            for q in range(1, RING):
                acc = acc + dot(oh[:, q * LANES : q * LANES + TOK], G[f][g][q * TOK : (q + 1) * TOK, cols])
            PK[f][g][:, cols] = acc.astype(BF16)
            return carry

        lax.fori_loop(0, width // 512, cols_step, 0)
        fold_out(PK[f][g], MAIN, es.at[f, g])

    def combine(f, g):
        lane = lax.broadcasted_iota(jnp.int32, (TOK, ROWS), 1)
        in_main = lane < MAIN
        block = jnp.where(in_main, lane // TOK, (lane - MAIN) // EXTRA)
        place = jnp.where(in_main, lax.rem(lane, TOK), TOK + lax.rem(lane - MAIN, EXTRA)).astype(F32)
        metas = (mo, mp)[g]
        for q in range(RING):
            m = jnp.concatenate([metas[f, q].astype(F32), jnp.zeros((LANES - 16, LANES), F32)], axis=0)
            m = m.T[0:TOK, :]
            s = m[:, 0:1]
            w = m[:, 4:5]
            for t in range(1, RING):
                s = jnp.where(block == t, m[:, t : t + 1], s)
                w = jnp.where(block == t, m[:, 4 + t : 5 + t], w)
            hit = jnp.logical_and(s >= 0, s + q * CAP == place)
            oh[q * TOK : (q + 1) * TOK, 0:ROWS] = jnp.where(hit, w, 0.0).astype(BF16)
        fold_in(yr.at[f, g], G[f][g], MAIN)

        def cols_step(j, carry):
            cols = aligned(j, 512)
            PK[f][g][0:MAIN, cols] = dot(oh[0:MAIN, 0:ROWS], G[f][g][:, cols]).astype(BF16)
            return carry

        lax.fori_loop(0, width // 512, cols_step, 0)

    def scatter_begin(f, g):
        axis, ref = AG_AXIS[g], PK[f][g]
        far = lax.rem(me[axis] + 2, RING)
        return [remote(slot_of(ref, far, LO), ra.at[f, g], peer(axis, 1)),
                remote(slot_of(ref, far, HI), rb.at[f, g], peer(axis, 3))]

    def scatter_relay(f, g, first):
        axis, ref = AG_AXIS[g], PK[f][g]
        m = me[axis]
        cps = []
        for i, (k, got, cols, dst) in enumerate(((1, ra, LO, rc), (3, rb, HI, rd))):
            first[i].wait_recv()
            c = lax.rem(m + k, RING)
            rows = pl.ds(pl.multiple_of(c * TOK, 16), TOK)
            ref[rows, cols] = (ref[rows, cols].astype(F32) + got[f, g].astype(F32)).astype(BF16)
            cps.append(remote(slot_of(ref, c), dst.at[f, g], peer(axis, k)))
        return cps

    def scatter_end(f, g, cps, more=None):
        axis, ref = AG_AXIS[g], PK[f][g]
        wait_recv(cps)
        rows = pl.ds(pl.multiple_of(me[axis] * TOK, 16), TOK)

        def cols_step(j, carry):
            cols = aligned(j, 512)
            acc = ref[rows, cols].astype(F32) + rc[f, g, :, cols].astype(F32) + rd[f, g, :, cols].astype(F32)
            if more is not None:
                acc = acc + more[:, cols].astype(F32)
            ref[rows, cols] = acc.astype(BF16)
            return carry

        lax.fori_loop(0, width // 512, cols_step, 0)

    own = [here(tok_hbm, slot_of(g_fo, y)), here(grd_hbm, slot_of(g_bo, y))]
    saved_in = [here(sg_hbm, hb.at[0 : TOK * 8, 0:inner]), here(su_hbm, hb.at[0 : TOK * 8, inner : 2 * inner])]
    begin(wa_pair)
    begin(wd_rows)

    barrier = pltpu.get_barrier_semaphore()
    everyone = [partner, next_sec, prev_sec] + [peer(a, k) for a in ("y", "x") for k in (1, 2, 3)]
    for device in everyone:
        pl.semaphore_signal(barrier, inc=1, device_id=device, device_id_type=MESH)
    pl.semaphore_wait(barrier, len(everyone))

    def tokens_begin(f):
        own[f].wait()
        to_z = remote(slot_of(G[f][O], y), slot_of(G[f][Q], x), partner)
        first = gather_begin("y", G[f][O])
        notes = [remote(meta.at[f, Q], mz.at[f], partner)]
        for k in (1, 2, 3):
            c = lax.rem(y + k, RING)
            notes.append(remote(meta.at[f, O, c], mo.at[f, y], at("y", c)))
        mo[f, y] = meta[f, O, y]
        return to_z, first, notes

    def partner_begin(f, to_z, notes):
        to_z.wait_recv()
        first = gather_begin("x", G[f][Q])
        notes[0].wait_recv()
        more = []
        for k in (1, 2, 3):
            c = lax.rem(x + k, RING)
            more.append(remote(mz.at[f, c], mp.at[f, x], at("x", c)))
        mp[f, x] = mz[f, x]
        return first, more

    def packed(f, g, sent, relays, notes):
        wait_recv(relays)
        wait_recv(notes)
        wait_send(sent + relays)
        pack(f, g)
        return exchange(UNI_AXIS[g], PK[f][g], 0, es.at[f, g], X[f], g * ROWS, er.at[f, g])

    z_f, o_f, n_f = tokens_begin(F)

    for cp in saved_in:
        cp.wait()
    for g, (dst, extra) in enumerate(((spk_o, spe.at[0]), (spk_p, spe.at[1]))):
        index = lax.broadcasted_iota(jnp.int32, (ROWS, TOK * 8), 0) + g * ROWS
        oh[...] = jnp.where(spos[...] == index, 1.0, 0.0).astype(BF16)

        def cols_step(j, carry):
            cols = aligned(j, 512)
            dst[:, cols] = dot(oh[...], hb[0 : TOK * 8, cols]).astype(BF16)
            return carry

        lax.fori_loop(0, 2 * inner // 512, cols_step, 0)
        fold_out(dst, MAIN, extra)

    ro_f = gather_relay("y", g_fo, o_f)
    p_f, np_f = partner_begin(F, z_f, n_f)
    z_b, o_b, n_b = tokens_begin(B)
    uo_f, lo_f = packed(F, O, [z_f] + o_f, ro_f, n_f[1:])
    s1_o, sl_o = exchange("y", spk_o, 0, spe.at[0], sg_o, 0, sge.at[0])
    s1_z = [remote(spk_p.at[0:MAIN, :], sz, partner), remote(spe.at[1], sze, partner)]
    rp_f = gather_relay("x", g_fp, p_f)
    ro_b = gather_relay("y", g_bo, o_b)
    up_f, lp_f = packed(F, Q, p_f, rp_f, np_f)
    p_b, np_b = partner_begin(B, z_b, n_b)
    wait_recv(s1_z)
    s1_p, sl_p = exchange("x", sz, 0, sze, sg_p, 0, sge.at[1])
    uo_b, lo_b = packed(B, O, [z_b] + o_b, ro_b, n_b[1:])
    rp_b = gather_relay("x", g_bp, p_b)

    def saved_second(g, first, own_copy, before, got, out):
        wait_recv(first)
        own_copy.wait()
        wait_send(before)
        fold_in(sge.at[g], got, MAIN)

        def cols_step(j, carry):
            cols = aligned(j, 512)
            out[:, cols] = dot(swap[...], got[:, cols]).astype(BF16)
            return carry

        lax.fori_loop(0, 2 * inner // 512, cols_step, 0)
        fold_out(out, MAIN, s2e.at[g])
        return exchange(UNI_AXIS[g], out, 0, s2e.at[g], sx, g * ROWS, sxe.at[g])

    s2_o, sm_o = saved_second(O, s1_o, sl_o, s1_o, sg_o, spk_o)
    up_b, lp_b = packed(B, Q, p_b, rp_b, np_b)
    s2_p, sm_p = saved_second(Q, s1_p, sl_p, s1_z, sg_p, spk_p)

    wait_recv(uo_f + up_f)
    lo_f.wait()
    lp_f.wait()
    for g in (O, Q):
        fold_in(er.at[F, g], x_f, g * ROWS + MAIN)

    def fwd_hidden(j, slot):
        for r in range(2):
            rows = slice(r * ROWS, (r + 1) * ROWS)
            both = dot(x_f[rows, :], wa[slot])
            gate, up = both[:, 0:LANES], both[:, LANES : 2 * LANES]
            hb[rows, aligned(j, LANES)] = (gate / (1.0 + jnp.exp(-gate)) * up).astype(BF16)

    stream(inner // LANES, wa_pair, fwd_hidden)
    begin(wa_down)

    def fwd_down(j, slot):
        for r in range(2):
            rows = slice(r * ROWS, (r + 1) * ROWS)
            x_f[rows, aligned(j, 256)] = dot(hb[rows, 0:inner], wa[slot, 0:inner, :]).astype(BF16)

    stream(width // 256, wa_down, fwd_down)

    def give_back(f):
        cps, owns = [], []
        for g in (O, Q):
            fold_out(X[f], g * ROWS + MAIN, ys.at[f, g])
            c, o = exchange(UNI_AXIS[g], X[f], g * ROWS, ys.at[f, g], G[f][g], 0, yr.at[f, g])
            cps.append(c)
            owns.append(o)
        return cps, owns

    back_f, own_f = give_back(F)

    wait_recv(uo_b + up_b + s2_o + s2_p)
    for cp in (lo_b, lp_b, sm_o, sm_p):
        cp.wait()
    for g in (O, Q):
        fold_in(er.at[B, g], x_b, g * ROWS + MAIN)
        fold_in(sxe.at[g], sx, g * ROWS + MAIN)

    def bwd_hidden(j, slot):
        cols, more = aligned(j, 256), pl.ds(pl.multiple_of(inner + j * 256, 256), 256)
        for r in range(2):
            rows = slice(r * ROWS, (r + 1) * ROWS)
            grad = dot_t(x_b[rows, :], wd_t[slot])
            a = sx[rows, cols].astype(F32)
            b = sx[rows, more].astype(F32)
            s = 1.0 / (1.0 + jnp.exp(-a))
            hb[rows, cols] = (grad * b * s * (1.0 + a * (1.0 - s))).astype(BF16)
            hb[rows, more] = (grad * a * s).astype(BF16)

    stream(inner // 256, wd_rows, bwd_hidden)
    begin(wd_pair)

    def bwd_down(j, slot):
        for r in range(2):
            rows = slice(r * ROWS, (r + 1) * ROWS)
            x_b[rows, aligned(j, 256)] = dot_t(hb[rows, :], wd_t[slot, :, 0 : 2 * inner]).astype(BF16)

    stream(width // 256, wd_pair, bwd_down)

    back_b, own_b = give_back(B)

    def sums_begin(f, g, back, own_copy, before):
        wait_recv(back)
        own_copy.wait()
        wait_send(before)
        combine(f, g)
        return scatter_begin(f, g)

    def sums(f, back, owns, before, out, device):
        first_p = sums_begin(f, Q, back[Q], owns[Q], before[Q])
        first_o = sums_begin(f, O, back[O], owns[O], before[O])
        second_p = scatter_relay(f, Q, first_p)
        second_o = scatter_relay(f, O, first_o)
        scatter_end(f, Q, second_p)
        home = remote(slot_of(PK[f][Q], x), zr.at[f], partner)
        home.wait_recv()
        scatter_end(f, O, second_o, zr.at[f])
        last = remote(slot_of(PK[f][O], y), out, device)
        return first_p + first_o + second_p + second_o + [home], last

    sent_f, last_f = sums(F, back_f, own_f, (uo_f, up_f), out_f, next_sec)
    sent_b, last_b = sums(B, back_b, own_b, (uo_b, up_b), out_b, prev_sec)

    wait_send(sent_f + sent_b + back_f[0] + back_f[1] + back_b[0] + back_b[1])
    wait_send(n_f + np_f + n_b + np_b + s1_p + s2_o + s2_p)
    last_f.wait()
    last_b.wait()


def place_notes(routes, gates, e):
    expert = jnp.arange(32, dtype=jnp.int32)
    hot = routes.T[None, :, :] == expert[:, None, None]
    named = jnp.any(hot, axis=1)
    count = named.astype(F32)
    earlier = jnp.asarray(np.triu(np.ones((TOK, TOK), np.float32), 1))
    within = jnp.dot(count, earlier, preferred_element_type=F32)
    slot = jnp.where(named, within, -1.0)
    gate = jnp.sum(jnp.where(hot, gates.T[None, :, :], 0.0), axis=1)
    z = e // 16
    out = []
    slots = slot.reshape(2, 4, 4, TOK)
    gates_ = gate.reshape(2, 4, 4, TOK)
    for plane, flip in ((z, False), (1 - z, True)):
        s = lax.dynamic_index_in_dim(slots, plane, 0, keepdims=False)
        w = lax.dynamic_index_in_dim(gates_, plane, 0, keepdims=False)
        if flip:
            s, w = s.transpose(1, 0, 2), w.transpose(1, 0, 2)
        both = jnp.concatenate([s, w, jnp.full((4, 8, TOK), -1.0, F32)], axis=1)
        out.append(jnp.pad(both, ((0, 0), (0, 0), (0, LANES - TOK)), constant_values=-1.0))
    return jnp.stack(out).astype(BF16), hot, within


def saved_places(routes, hot, within, e):
    slot = jnp.sum(jnp.where(hot, within[:, None, :], 0.0), axis=0).T.astype(jnp.int32)
    z = e // 16
    there, ey, ex = routes // 16, lax.rem(routes // 4, 4), lax.rem(routes, 4)
    same = there == z
    block = jnp.where(same, ey, ex)
    place = jnp.where(same, ex, ey) * CAP + slot
    row = jnp.where(place < TOK, block * TOK + place, MAIN + block * EXTRA + place - TOK)
    return (row + jnp.where(same, 0, ROWS)).reshape(1, -1)


def body(
    fwd_tokens,
    fwd_routes,
    fwd_gates,
    bwd_grads,
    bwd_routes,
    bwd_gates,
    saved_gate,
    saved_up,
    w_gate,
    w_up,
    w_down,
):
    e = lax.axis_index("expert")
    tokens, grads = fwd_tokens[0], bwd_grads[0]
    width, inner = tokens.shape[1], w_gate.shape[3]
    note_f, _, _ = place_notes(fwd_routes[0], fwd_gates[0], e)
    note_b, hot, within = place_notes(bwd_routes[0], bwd_gates[0], e)
    meta = jnp.stack([note_f, note_b])
    spos = saved_places(bwd_routes[0], hot, within, e)
    quarter = width // 4
    any_, vmem = pl.BlockSpec(memory_space=pl.ANY), pl.BlockSpec(memory_space=pltpu.VMEM)

    def buf(*shape):
        return pltpu.VMEM(shape, BF16)

    scratch = (
        [buf(ROWS, width)] * 8
        + [buf(2 * ROWS, width)] * 2
        + [buf(2, 2, 4 * TAIL, quarter)] * 4
        + [buf(2, 2, TOK, width // 2)] * 2
        + [buf(2, 2, TOK, width)] * 2
        + [buf(2, TOK, width)]
        + [buf(2, 4, 16, LANES)] * 3
        + [buf(ROWS, 2 * inner)] * 4
        + [buf(MAIN, 2 * inner), buf(2 * ROWS, 2 * inner)]
        + [buf(2, 4 * TAIL, inner // 2)] * 2
        + [buf(4 * TAIL, inner // 2)]
        + [buf(2, 4 * TAIL, inner // 2)] * 2
        + [buf(2 * ROWS, 2 * inner), buf(ROWS, TOK * 8)]
        + [buf(2, width, 256), buf(2, 256, width)]
        + [pltpu.SemaphoreType.DMA((N_SEMS,)), pltpu.SemaphoreType.DMA((N_SEMS,))]
        + [pltpu.SemaphoreType.DMA((N_LOCAL,)), pltpu.SemaphoreType.DMA((4, 2))]
    )
    out = jax.ShapeDtypeStruct(tokens.shape, BF16)
    rows = 2 * ROWS
    next_inputs, prev_grads = pl.pallas_call(
        kernel,
        out_shape=(out, out),
        in_specs=[any_] * 7 + [vmem] * 4,
        out_specs=(any_, any_),
        scratch_shapes=scratch,
        compiler_params=pltpu.CompilerParams(
            collective_id=1, has_side_effects=True, vmem_limit_bytes=62 * 1024 * 1024
        ),
        cost_estimate=pl.CostEstimate(
            flops=12 * rows * width * inner, bytes_accessed=12 * width * inner, transcendentals=2 * rows * inner
        ),
    )(
        tokens,
        grads,
        saved_gate[0].reshape(-1, inner),
        saved_up[0].reshape(-1, inner),
        w_gate[0, 0],
        w_up[0, 0],
        w_down[0, 0],
        meta,
        spos,
        jnp.asarray(fold_matrix(), BF16),
        jnp.asarray(swap_matrix(), BF16),
    )
    return (next_inputs[None], prev_grads[None])


def solution(mesh):
    return jax.shard_map(
        body,
        mesh=mesh,
        in_specs=(P("section", "expert", None),) * 6 + (P("section", "expert", None, None),) * 5,
        out_specs=(P("section", "expert", None), P("section", "expert", None)),
        check_vma=False,
    )
```

time: 437 us -> 320 us (0.73)
  Pallas kernels: 0 us -> 302 us
  waiting for transfers between devices: 179 us -> 0 us
  local copies, waits for them, and re-layouts: 118 us -> 4.73 us
  matrix products: 53.4 us -> 1.71 us
  starting transfers between devices: 46.8 us -> 0 us
  other arithmetic: 29.8 us -> 4.45 us
    pallas_call x0 -> x1, Pallas kernels: none -> 302 us  [body(): pl.pallas_call(kernel, out_shape=(out, out), in_specs=[any_] * 7 + [vmem]...]
    all_to_all x6 -> x0, waiting for transfers between devices: 169 us -> none  [the longest x1 46.4 us: body(): lax.all_to_all(send_grad, 'expert', split_axis=1, concat_axis=1, tiled=True)]
    dot_general x5 -> x2, matrix products: 53.4 us -> 1.71 us  [place_notes(): within = jnp.dot(count, earlier, preferred_element_type=F32)]
    all_to_all x6 -> x0, starting transfers between devices: 44.6 us -> none  [the longest x1 8.86 us: body(): lax.all_to_all(send_gate, 'expert', split_axis=1, concat_axis=1, tiled=True)]
    reshape x6 -> x1, local copies, waits for them, and re-layouts: 32.5 us -> 0.67 us  [saved_places(): return (row + jnp.where(same, 0, ROWS)).reshape(1, -1)]
    gather x2 -> x0, local copies, waits for them, and re-layouts: 27.4 us -> none  [the longest x1 13.8 us: body(): back_fwd.reshape(capacity * groups, width)[fwd_dest].astype(jnp.float32)]
    scatter x3 -> x0, local copies, waits for them, and re-layouts: 27 us -> none  [the longest x1 13.3 us: body(): send_fwd = jnp.zeros((capacity * groups, width), jnp.bfloat16).at[flat_fw...]
    all_to_all x6 -> x0, local copies, waits for them, and re-layouts: 24.7 us -> none  [the longest x1 6.21 us: body(): lax.all_to_all(fwd_rows.reshape(slots_here, groups, width), 'expert', spl...]
  transfers between devices with their start and end apart: 8 -> 0, of which waited for: 6 -> 0; matrix products, arithmetic and copies ran while one was open for 43% -> 0% of each run, Pallas kernels for 0% -> 0%
where the time goes in v1:
time: 320 us; the launch traced here: 313 us
  Pallas kernels  302 us (94%)
  local copies, waits for them, and re-layouts  4.73 us (1%)
  other arithmetic  4.45 us (1%)
    pallas_call x1, Pallas kernels, body(): pl.pallas_call(kernel, out_shape=(out, out), in_specs=[any_] * 7 + [vmem]...  302 us

profile of v1, /device:TPU:10, one launch (start us, length us, event | category | flops | bytes accessed | tf_op | source)
XLA Modules:
  0.0 313.4 jit_solution(10943035000036878485)
XLA Ops:
  0.7 0.1 pad.36.clone
  0.7 0.7 fusion.1
  1.5 0.9 convolution_select_fusion
  2.3 0.7 fusion
  3.1 0.8 select_reduce_fusion.2
  3.9 0.9 broadcast_select_fusion
  4.7 0.8 select_reduce_fusion
  5.5 0.7 select_add_fusion
  6.3 0.1 maximum_maximum_fusion.1
  6.4 0.6 maximum_maximum_fusion.meta
  7.1 0.1 copy.31
  7.2 0.7 reshape.94.spos
  7.8 301.8 %shard_map.158 = (bf16[80,3584]{1,0:T(8,128)(2,1)}, bf16[80,3584]{1,0:T(8,128)(2,1)}) custom-call(bf16[80,3584]{1,0:T(8,128)(2,1)} %bitcast.103, bf16[80,3584]{1,0:T(8,128)(2,1)} %bitcast.104, bf16[640,1024]{1,0:T(8,128)(2,1)} %bitcast.101, bf16[640,1024]{1,0:T(8,128)(2,1)} %bitcast.102, bf16[3584,1024]{1,0:T(8,128)(2,1)} %bitcast.98, ...), custom_call_target="tpu_custom_call" | custom-call | flops 29595009024 | bytes 44040192 | tf_op jit(solution)/shard_map/pallas_call | solution.py:578
  309.6 1.9 copy.34
  311.5 1.9 copy.35
  (11 shorter events, 0.1 us)

commit v2 on v1

v2 whole, which is shorter than its diff:
```python
import functools

import jax
import jax.numpy as jnp
import numpy as np
from jax import lax
from jax.experimental import pallas as pl
from jax.experimental.pallas import tpu as pltpu
from jax.sharding import PartitionSpec as P

MESH = pl.DeviceIdType.MESH
F32 = jnp.float32
BF16 = jnp.bfloat16

RING = 4
CAP = 21
TOK = 80
GROUP = RING * CAP
EXTRA = GROUP - TOK
MAIN = RING * TOK
ROWS = RING * GROUP
TAIL = ROWS - MAIN
LANES = 128
N_SEMS = 176
N_LOCAL = 24


def row_of(block, place):
    return block * TOK + place if place < TOK else MAIN + block * EXTRA + place - TOK


def swap_matrix():
    m = np.zeros((ROWS, ROWS), np.float32)
    for q in range(RING):
        for t in range(RING):
            for i in range(CAP):
                m[row_of(t, q * CAP + i), row_of(q, t * CAP + i)] = 1
    return m


def fold_matrix():
    m = np.zeros((4 * TAIL, 4 * TAIL), np.float32)
    for a in range(4):
        for b in range(4):
            for j in range(4):
                m[b * 16 + a * 4 + j, a * 16 + b * 4 + j] = 1
    return m


def dot(a, b):
    return jnp.dot(a, b, preferred_element_type=F32)


def dot_t(a, b):
    return lax.dot_general(a, b, (((1,), (1,)), ((), ())), preferred_element_type=F32)


def aligned(i, size):
    return pl.ds(pl.multiple_of(i * size, size), size)


def kernel(
    tok_hbm,
    grd_hbm,
    sg_hbm,
    su_hbm,
    wg_hbm,
    wu_hbm,
    wd_hbm,
    routes_f, gates_f, routes_b, gates_b,
    fold,
    swap,
    out_fo, out_fp, out_bo, out_bp,
    g_fo, g_fp, g_bo, g_bp,
    pk_fo, pk_fp, pk_bo, pk_bp,
    x_f, x_b,
    es, er, ys, yr,
    ra, rb, rc, rd, zr,
    meta, mo, mz, mp, turn, spos,
    spk_o, spk_p, sg_o, sg_p, sz, sx,
    spe, sge, sze, s2e, sxe,
    hb, oh, qm, gc, wa, wd_t,
    send, recv, local, wsem,
):
    e = lax.axis_index("expert")
    sec = lax.axis_index("section")
    n_sec = lax.axis_size("section")
    z, y, x = e // 16, lax.rem(e // 4, 4), lax.rem(e, 4)
    me = {"y": y, "x": x}
    width = tok_hbm.shape[1]
    inner = wg_hbm.shape[1]
    half = width // 2
    F, B, O, Q = 0, 1, 0, 1
    G = ((g_fo, g_fp), (g_bo, g_bp))
    PK = ((pk_fo, pk_fp), (pk_bo, pk_bp))
    X = (x_f, x_b)
    AG_AXIS = (("y", "x"), ("x", "y"))
    UNI_AXIS = (("x", "y"), ("y", "x"))
    CHUNKS = ((0, 2048), (2048, width - 2048))

    def at(axis, c):
        if axis == "y":
            return (sec, z * 16 + c * 4 + x)
        return (sec, z * 16 + y * 4 + c)

    def peer(axis, k):
        return at(axis, lax.rem(me[axis] + k, RING))

    other = (1 - z) * 16 + y * 4 + x
    partner = (sec, other)
    next_sec = lax.rem(sec + 1, n_sec)
    prev_sec = lax.rem(sec + n_sec - 1, n_sec)

    used = [0, 0]

    def remote(src, dst, device):
        i = used[0]
        used[0] += 1
        cp = pltpu.make_async_remote_copy(
            src_ref=src, dst_ref=dst, send_sem=send.at[i], recv_sem=recv.at[i],
            device_id=device, device_id_type=MESH,
        )
        cp.start()
        return cp

    def here(src, dst):
        i = used[1]
        used[1] += 1
        cp = pltpu.make_async_copy(src, dst, local.at[i])
        cp.start()
        return cp

    def wait_recv(cps):
        for cp in cps:
            cp.wait_recv()

    def wait_send(cps):
        for cp in cps:
            cp.wait_send()

    def turned(ref, fill):
        turn[...] = jnp.full((8, LANES), fill, F32)
        turn[:, 0:TOK] = ref[...].astype(F32)
        return turn[...]

    def places(f, routes, gates):
        named_by = turned(routes, -1.0)
        gate_by = turned(gates, 0.0)
        expert = lax.broadcasted_iota(jnp.int32, (32, LANES), 0).astype(F32)
        hot = [named_by[k : k + 1, :] == expert for k in range(8)]
        count = jnp.zeros((32, LANES), F32)
        gate = jnp.zeros((32, LANES), F32)
        for k in range(8):
            count += jnp.where(hot[k], 1.0, 0.0)
            gate += jnp.where(hot[k], gate_by[k : k + 1, :], 0.0)
        earlier = lax.broadcasted_iota(jnp.int32, (LANES, LANES), 0) < lax.broadcasted_iota(jnp.int32, (LANES, LANES), 1)
        within = dot(count.astype(BF16), jnp.where(earlier, 1.0, 0.0).astype(BF16))
        high = gate.astype(BF16).astype(F32)
        rows = jnp.concatenate([jnp.where(count > 0, within, -1.0), high, gate - high], axis=0).astype(BF16)
        r = lax.broadcasted_iota(jnp.int32, (64, 96), 0)
        message, kind, item = r // 16, lax.rem(r, 16) // 4, lax.rem(r, 4)
        col = lax.broadcasted_iota(jnp.int32, (64, 96), 1)
        for g in (O, Q):
            plane = z if g == O else 1 - z
            if AG_AXIS[f][g] == "y":
                index = plane * 16 + message * 4 + item
            else:
                index = plane * 16 + item * 4 + message
            pick = jnp.where(jnp.logical_and(kind < 3, col == kind * 32 + index), 1.0, 0.0).astype(BF16)
            got = dot(pick, rows).astype(BF16)
            for c in range(4):
                meta[f, g, c] = got[c * 16 : (c + 1) * 16, :]
        if f == F:
            return
        slot = jnp.concatenate(
            [jnp.sum(jnp.where(hot[k], within, 0.0), axis=0, keepdims=True) for k in range(8)], axis=0
        ).astype(jnp.int32)
        chosen = named_by.astype(jnp.int32)
        same = chosen // 16 == z
        cy, cx = lax.rem(chosen // 4, 4), lax.rem(chosen, 4)
        block = jnp.where(same, cx, cy)
        place = jnp.where(same, cy, cx) * CAP + slot
        row = jnp.where(place < TOK, block * TOK + place, MAIN + block * EXTRA + place - TOK)
        row = row + jnp.where(same, 0, ROWS)
        token = lax.broadcasted_iota(jnp.int32, (LANES, TOK * 8), 0)
        lane = lax.broadcasted_iota(jnp.int32, (LANES, TOK * 8), 1)
        spread = jnp.where(lane // 8 == token, 1.0, 0.0).astype(BF16)
        coarse = (row // 16).astype(F32).astype(BF16)
        fine = lax.rem(row, 16).astype(F32).astype(BF16)
        wide = 16.0 * dot(coarse, spread) + dot(fine, spread)
        mine = lax.broadcasted_iota(jnp.int32, (8, TOK * 8), 0) == lax.rem(lane[0:8, :], 8)
        total = jnp.sum(jnp.where(mine, wide, 0.0), axis=0, keepdims=True)
        spos[...] = jnp.broadcast_to(total, (8, TOK * 8))

    def wa_pair(j, slot):
        cols = pl.ds(pl.multiple_of(j * LANES, LANES), LANES)
        return (
            pltpu.make_async_copy(wg_hbm.at[:, cols], wa.at[slot, :, 0:LANES], wsem.at[0, slot]),
            pltpu.make_async_copy(wu_hbm.at[:, cols], wa.at[slot, :, LANES : 2 * LANES], wsem.at[1, slot]),
        )

    def wa_down(j, slot):
        cols = pl.ds(pl.multiple_of(j * 256, 256), 256)
        return (pltpu.make_async_copy(wd_hbm.at[:, cols], wa.at[slot, 0:inner, :], wsem.at[0, slot]),)

    def wd_rows(j, slot):
        rows = aligned(j, 256)
        return (pltpu.make_async_copy(wd_hbm.at[rows, :], wd_t.at[slot], wsem.at[2, slot]),)

    def wd_pair(j, slot):
        rows = aligned(j, 256)
        return (
            pltpu.make_async_copy(wg_hbm.at[rows, :], wd_t.at[slot, :, 0:inner], wsem.at[2, slot]),
            pltpu.make_async_copy(wu_hbm.at[rows, :], wd_t.at[slot, :, inner : 2 * inner], wsem.at[3, slot]),
        )

    def begin(tiles):
        for cp in tiles(0, 0):
            cp.start()

    def stream(n, tiles, work, first=0, last=None):
        def step(j, carry):
            slot = lax.rem(j, 2)

            @pl.when(j + 1 < n)
            def _():
                for cp in tiles(j + 1, 1 - slot):
                    cp.start()

            for cp in tiles(j, slot):
                cp.wait()
            work(j, slot)
            return carry

        lax.fori_loop(first, n if last is None else last, step, 0)

    def fold_out(src, row0, dst, col0=0, size=None):
        w4 = (src.shape[1] if size is None else size) // 4
        a = jnp.concatenate(
            [src[row0 : row0 + TAIL, col0 + c * w4 : col0 + (c + 1) * w4] for c in range(4)], axis=0)
        dst[...] = dot(fold[...], a).astype(BF16)

    def fold_in(src, dst, row0, col0=0, size=None):
        w4 = (dst.shape[1] if size is None else size) // 4
        a = dot(fold[...], src[...]).astype(BF16)
        for c in range(4):
            dst[row0 : row0 + TAIL, col0 + c * w4 : col0 + (c + 1) * w4] = a[c * TAIL : (c + 1) * TAIL, :]

    def exchange(axis, src, src_off, src_extra, dst, dst_off, dst_extra, cols=slice(None)):
        m = me[axis]
        cps = []
        for k in (2, 1, 3):
            c = lax.rem(m + k, RING)
            cps.append(remote(
                src.at[pl.ds(pl.multiple_of(src_off + c * TOK, 16), TOK), cols],
                dst.at[pl.ds(pl.multiple_of(dst_off + m * TOK, 16), TOK), cols],
                at(axis, c)))
            cps.append(remote(src_extra.at[aligned(c, TAIL), :], dst_extra.at[aligned(m, TAIL), :], at(axis, c)))
        own = here(
            src.at[pl.ds(pl.multiple_of(src_off + m * TOK, 16), TOK), cols],
            dst.at[pl.ds(pl.multiple_of(dst_off + m * TOK, 16), TOK), cols])
        dst_extra[aligned(m, TAIL), :] = src_extra[aligned(m, TAIL), :]
        return cps, own

    def slot_of(ref, c, cols=None):
        rows = pl.ds(pl.multiple_of(c * TOK, 16), TOK)
        return ref.at[rows, :] if cols is None else ref.at[rows, cols]

    LO, HI = pl.ds(0, half), pl.ds(half, half)

    def gather_begin(axis, ref):
        m = me[axis]
        return [remote(slot_of(ref, m), slot_of(ref, m), peer(axis, 1)),
                remote(slot_of(ref, m), slot_of(ref, m), peer(axis, 3))]

    def gather_relay(axis, ref, first):
        m = me[axis]
        before, after = lax.rem(m + 3, RING), lax.rem(m + 1, RING)
        first[0].wait_recv()
        a = remote(slot_of(ref, before, LO), slot_of(ref, before, LO), peer(axis, 1))
        first[1].wait_recv()
        b = remote(slot_of(ref, after, HI), slot_of(ref, after, HI), peer(axis, 3))
        return [a, b]

    def pack(f, g):
        wide = lax.broadcasted_iota(jnp.int32, (TOK, LANES), 0).astype(F32)
        tail = lax.broadcasted_iota(jnp.int32, (TAIL, LANES), 0)
        tail_place = (TOK + lax.rem(tail, EXTRA)).astype(F32)
        tail_block = tail // EXTRA
        metas = (mo, mp)[g]
        gate = [jnp.zeros((TOK, 1), F32)] * RING
        tail_gate = jnp.zeros((TAIL, 1), F32)
        for q in range(RING):
            m = metas[f, q].astype(F32)
            s = jnp.where(m >= 0, m + q * CAP, -1.0)
            w = m[4:8, :] + m[8:12, :]
            cols = slice(q * LANES, (q + 1) * LANES)
            chosen = jnp.zeros((TAIL, LANES), F32)
            weight = jnp.zeros((TAIL, LANES), F32)
            for t in range(RING):
                row, w_row = s[t : t + 1, :], w[t : t + 1, :]
                hit = wide == row
                oh[t * TOK : (t + 1) * TOK, cols] = jnp.where(hit, 1.0, 0.0).astype(BF16)
                chosen = jnp.where(tail_block == t, row, chosen)
                if f == B:
                    gate[t] += jnp.sum(jnp.where(hit, w_row, 0.0), axis=1, keepdims=True)
                    weight = jnp.where(tail_block == t, w_row, weight)
            hit = chosen == tail_place
            oh[MAIN:ROWS, cols] = jnp.where(hit, 1.0, 0.0).astype(BF16)
            tail_gate += jnp.sum(jnp.where(hit, weight, 0.0), axis=1, keepdims=True)
        if f == B:
            for t in range(RING):
                gc[t * TOK : (t + 1) * TOK, :] = jnp.broadcast_to(gate[t], (TOK, LANES))
            gc[MAIN:ROWS, :] = jnp.broadcast_to(tail_gate, (TAIL, LANES))

        def cols_step(j, carry):
            cols = aligned(j, 512)
            acc = dot(oh[:, 0:TOK], G[f][g][0:TOK, cols])
            for q in range(1, RING):
                acc = acc + dot(oh[:, q * LANES : q * LANES + TOK], G[f][g][q * TOK : (q + 1) * TOK, cols])
            if f == B:
                acc = acc * gc[:, 0:1]
            PK[f][g][:, cols] = acc.astype(BF16)
            return carry

        lax.fori_loop(0, width // 512, cols_step, 0)
        fold_out(PK[f][g], MAIN, es.at[f, g])

    def weights(f, g):
        lane = lax.broadcasted_iota(jnp.int32, (TOK, ROWS), 1)
        in_main = lane < MAIN
        block = jnp.where(in_main, lane // TOK, (lane - MAIN) // EXTRA)
        place = jnp.where(in_main, lax.rem(lane, TOK), TOK + lax.rem(lane - MAIN, EXTRA)).astype(F32)
        metas = (mo, mp)[g]
        for q in range(RING):
            m = jnp.concatenate([metas[f, q].astype(F32), jnp.zeros((LANES - 16, LANES), F32)], axis=0)
            m = m.T[0:TOK, :]
            s = m[:, 0:1]
            w = m[:, 4:5]
            for t in range(1, RING):
                s = jnp.where(block == t, m[:, t : t + 1], s)
                w = jnp.where(block == t, m[:, 4 + t : 5 + t], w)
            hit = jnp.logical_and(s >= 0, s + q * CAP == place)
            qm[f, g, q * TOK : (q + 1) * TOK, :] = jnp.where(hit, w if f == F else 1.0, 0.0).astype(BF16)

    def combine(f, g, h):
        col0, size = CHUNKS[h]
        fold_in(yr.at[f, g, :, pl.ds(col0 // 4, size // 4)], G[f][g], MAIN, col0, size)

        def cols_step(j, carry):
            cols = aligned(j, 512)
            PK[f][g][0:MAIN, cols] = dot(qm[f, g], G[f][g][:, cols]).astype(BF16)
            return carry

        lax.fori_loop(col0 // 512, (col0 + size) // 512, cols_step, 0)

    def parts(h):
        col0, size = CHUNKS[h]
        return (pl.ds(col0, size // 2), pl.ds(col0 + size // 2, size // 2)), pl.ds(col0 // 2, size // 2), pl.ds(col0, size)

    def scatter_begin(f, g, h):
        axis, ref = AG_AXIS[f][g], PK[f][g]
        (lo, hi), short, _ = parts(h)
        far = lax.rem(me[axis] + 2, RING)
        return [remote(slot_of(ref, far, lo), ra.at[f, g, :, short], peer(axis, 1)),
                remote(slot_of(ref, far, hi), rb.at[f, g, :, short], peer(axis, 3))]

    def scatter_relay(f, g, h, first):
        axis, ref = AG_AXIS[f][g], PK[f][g]
        ends, short, whole = parts(h)
        m = me[axis]
        cps = []
        for i, (k, got, dst) in enumerate(((1, ra, rc), (3, rb, rd))):
            first[i].wait_recv()
            c = lax.rem(m + k, RING)
            rows = pl.ds(pl.multiple_of(c * TOK, 16), TOK)
            ref[rows, ends[i]] = (ref[rows, ends[i]].astype(F32) + got[f, g, :, short].astype(F32)).astype(BF16)
            cps.append(remote(slot_of(ref, c, whole), dst.at[f, g, :, whole], peer(axis, k)))
        return cps

    def scatter_end(f, g, h, cps, out, device):
        axis, ref = AG_AXIS[f][g], PK[f][g]
        col0, size = CHUNKS[h]
        wait_recv(cps)
        rows = pl.ds(pl.multiple_of(me[axis] * TOK, 16), TOK)

        def cols_step(j, carry):
            cols = aligned(j, 512)
            acc = ref[rows, cols].astype(F32) + rc[f, g, :, cols].astype(F32) + rd[f, g, :, cols].astype(F32)
            ref[rows, cols] = acc.astype(BF16)
            return carry

        lax.fori_loop(col0 // 512, (col0 + size) // 512, cols_step, 0)
        whole = pl.ds(col0, size)
        return remote(slot_of(ref, me[axis], whole), out.at[:, whole], device)

    own = [here(tok_hbm, slot_of(g_fo, y)), here(grd_hbm, slot_of(g_bo, x))]
    saved_in = [here(sg_hbm, hb.at[0 : TOK * 8, 0:inner]), here(su_hbm, hb.at[0 : TOK * 8, inner : 2 * inner])]
    begin(wa_pair)
    begin(wd_rows)

    barrier = pltpu.get_barrier_semaphore()
    everyone = [partner, (next_sec, e), (prev_sec, e), (next_sec, other), (prev_sec, other)]
    everyone += [peer(a, k) for a in ("y", "x") for k in (1, 2, 3)]
    for device in everyone:
        pl.semaphore_signal(barrier, inc=1, device_id=device, device_id_type=MESH)
    pl.semaphore_wait(barrier, len(everyone))

    def gather_first(f):
        own[f].wait()
        return gather_begin(AG_AXIS[f][O], G[f][O])

    def partner_send(f):
        return remote(slot_of(G[f][O], me[AG_AXIS[f][O]]), slot_of(G[f][Q], me[AG_AXIS[f][Q]]), partner)

    def notes_begin(f):
        axis = AG_AXIS[f][O]
        m = me[axis]
        notes = [remote(meta.at[f, Q], mz.at[f], partner)]
        for k in (1, 2, 3):
            c = lax.rem(m + k, RING)
            notes.append(remote(meta.at[f, O, c], mo.at[f, m], at(axis, c)))
        mo[f, m] = meta[f, O, m]
        return notes

    def partner_begin(f, to_z, notes):
        axis = AG_AXIS[f][Q]
        m = me[axis]
        to_z.wait_recv()
        first = gather_begin(axis, G[f][Q])
        notes[0].wait_recv()
        more = []
        for k in (1, 2, 3):
            c = lax.rem(m + k, RING)
            more.append(remote(mz.at[f, c], mp.at[f, m], at(axis, c)))
        mp[f, m] = mz[f, m]
        return first, more

    def packed(f, g, sent, relays, notes):
        wait_recv(notes)
        wait_recv(relays)
        wait_send(sent + relays)
        pack(f, g)
        return exchange(UNI_AXIS[f][g], PK[f][g], 0, es.at[f, g], X[f], g * ROWS, er.at[f, g])

    def saved_pack(g, dst):
        index = (lax.broadcasted_iota(jnp.int32, (ROWS, TOK * 8), 0) + g * ROWS).astype(F32)
        oh[...] = jnp.where(spos[0:1, :] == index, 1.0, 0.0).astype(BF16)

        def cols_step(j, carry):
            cols = aligned(j, 512)
            dst[:, cols] = dot(oh[...], hb[0 : TOK * 8, cols]).astype(BF16)
            return carry

        lax.fori_loop(0, 2 * inner // 512, cols_step, 0)
        fold_out(dst, MAIN, spe.at[g])

    o_f = gather_first(F)
    z_f = partner_send(F)
    o_b = gather_first(B)
    places(F, routes_f, gates_f)
    n_f = notes_begin(F)
    places(B, routes_b, gates_b)
    n_b = notes_begin(B)
    for cp in saved_in:
        cp.wait()
    saved_pack(Q, spk_p)
    ro_f = gather_relay("y", g_fo, o_f)
    ro_b = gather_relay("x", g_bo, o_b)
    p_f, np_f = partner_begin(F, z_f, n_f)
    z_b = partner_send(B)
    uo_f, lo_f = packed(F, O, [z_f] + o_f, ro_f, n_f[1:])
    uo_b, lo_b = packed(B, O, [z_b] + o_b, ro_b, n_b[1:])
    p_b, np_b = partner_begin(B, z_b, n_b)
    s1_z = [remote(spk_p.at[0:MAIN, :], sz, partner), remote(spe.at[1], sze, partner)]
    rp_f = gather_relay("x", g_fp, p_f)
    saved_pack(O, spk_o)
    s1_o, sl_o = exchange("x", spk_o, 0, spe.at[0], sg_o, 0, sge.at[0])
    weights(F, O)
    up_f, lp_f = packed(F, Q, p_f, rp_f, np_f)
    rp_b = gather_relay("y", g_bp, p_b)
    weights(F, Q)
    up_b, lp_b = packed(B, Q, p_b, rp_b, np_b)
    wait_recv(s1_z)
    s1_p, sl_p = exchange("y", sz, 0, sze, sg_p, 0, sge.at[1])

    def saved_second(g, first, own_copy, before, got, out):
        wait_recv(first)
        own_copy.wait()
        wait_send(before)
        fold_in(sge.at[g], got, MAIN)

        def cols_step(j, carry):
            cols = aligned(j, 512)
            out[:, cols] = dot(swap[...], got[:, cols]).astype(BF16)
            return carry

        lax.fori_loop(0, 2 * inner // 512, cols_step, 0)
        fold_out(out, MAIN, s2e.at[g])
        return exchange(UNI_AXIS[B][g], out, 0, s2e.at[g], sx, g * ROWS, sxe.at[g])

    s2_o, sm_o = saved_second(O, s1_o, sl_o, s1_o, sg_o, spk_o)
    weights(B, O)
    weights(B, Q)

    wait_recv(uo_f + up_f)
    lo_f.wait()
    lp_f.wait()
    for g in (O, Q):
        fold_in(er.at[F, g], x_f, g * ROWS + MAIN)

    def fwd_hidden(j, slot):
        for r in range(2):
            rows = slice(r * ROWS, (r + 1) * ROWS)
            both = dot(x_f[rows, :], wa[slot])
            gate, up = both[:, 0:LANES], both[:, LANES : 2 * LANES]
            hb[rows, aligned(j, LANES)] = (gate / (1.0 + jnp.exp(-gate)) * up).astype(BF16)

    stream(inner // LANES, wa_pair, fwd_hidden)
    begin(wa_down)
    s2_p, sm_p = saved_second(Q, s1_p, sl_p, s1_z, sg_p, spk_p)

    def fwd_down(j, slot):
        for r in range(2):
            rows = slice(r * ROWS, (r + 1) * ROWS)
            x_f[rows, aligned(j, 256)] = dot(hb[rows, 0:inner], wa[slot, 0:inner, :]).astype(BF16)

    def give_back(f, h):
        col0, size = CHUNKS[h]
        cps, owns = [], []
        for g in (Q, O):
            extra = (f, g, slice(None), pl.ds(col0 // 4, size // 4))
            fold_out(X[f], g * ROWS + MAIN, ys.at[extra], col0, size)
            c, o = exchange(
                UNI_AXIS[f][g], X[f], g * ROWS, ys.at[extra], G[f][g], 0, yr.at[extra], pl.ds(col0, size))
            cps = cps + c
            owns.append(o)
        return cps, owns

    tiles = width // 256
    cut = CHUNKS[0][1] // 256
    stream(tiles, wa_down, fwd_down, 0, cut)
    back_f0 = give_back(F, 0)
    stream(tiles, wa_down, fwd_down, cut, tiles)
    back_f1 = give_back(F, 1)

    wait_recv(uo_b + up_b + s2_o + s2_p)
    for cp in (lo_b, lp_b, sm_o, sm_p):
        cp.wait()
    for g in (O, Q):
        fold_in(er.at[B, g], x_b, g * ROWS + MAIN)
        fold_in(sxe.at[g], sx, g * ROWS + MAIN)

    def bwd_hidden(j, slot):
        cols, more = aligned(j, 256), pl.ds(pl.multiple_of(inner + j * 256, 256), 256)
        for r in range(2):
            rows = slice(r * ROWS, (r + 1) * ROWS)
            grad = dot_t(x_b[rows, :], wd_t[slot])
            a = sx[rows, cols].astype(F32)
            b = sx[rows, more].astype(F32)
            s = 1.0 / (1.0 + jnp.exp(-a))
            hb[rows, cols] = (grad * b * s * (1.0 + a * (1.0 - s))).astype(BF16)
            hb[rows, more] = (grad * a * s).astype(BF16)

    stream(inner // 256, wd_rows, bwd_hidden)
    begin(wd_pair)

    def bwd_down(j, slot):
        for r in range(2):
            rows = slice(r * ROWS, (r + 1) * ROWS)
            x_b[rows, aligned(j, 256)] = dot_t(hb[rows, :], wd_t[slot, :, 0 : 2 * inner]).astype(BF16)

    def sums_begin(f, h, back, before):
        cps, owns = back
        wait_recv(cps)
        for cp in owns:
            cp.wait()
        wait_send(before)
        first = {}
        for g in (Q, O):
            combine(f, g, h)
            first[g] = scatter_begin(f, g, h)
        return first

    def sums_relay(f, h, first):
        return {g: scatter_relay(f, g, h, first[g]) for g in (Q, O)}

    outs = ((out_fo, out_fp), (out_bo, out_bp))
    to_sec = (next_sec, prev_sec)

    def sums_end(f, h, second):
        return [scatter_end(f, g, h, second[g], outs[f][g], (to_sec[f], (e, other)[g])) for g in (Q, O)]

    sent, last = [], []

    def note(cps):
        for g in (Q, O):
            sent.extend(cps[g])
        return cps

    stream(tiles, wd_pair, bwd_down, 0, cut)
    back_b0 = give_back(B, 0)
    f0 = note(sums_begin(F, 0, back_f0, uo_f + up_f))
    stream(tiles, wd_pair, bwd_down, cut, tiles)
    back_b1 = give_back(B, 1)
    f1 = note(sums_begin(F, 1, back_f1, []))
    f0 = note(sums_relay(F, 0, f0))
    f1 = note(sums_relay(F, 1, f1))
    last += sums_end(F, 0, f0)
    b0 = note(sums_begin(B, 0, back_b0, uo_b + up_b))
    last += sums_end(F, 1, f1)
    b0 = note(sums_relay(B, 0, b0))
    b1 = note(sums_begin(B, 1, back_b1, []))
    last += sums_end(B, 0, b0)
    b1 = note(sums_relay(B, 1, b1))
    last += sums_end(B, 1, b1)

    wait_send(sent + back_f0[0] + back_f1[0] + back_b0[0] + back_b1[0])
    wait_send(n_f + np_f + n_b + np_b + s1_p + s2_o + s2_p)
    for cp in last:
        cp.wait()
    assert used[0] <= N_SEMS and used[1] <= N_LOCAL, used


def body(
    fwd_tokens,
    fwd_routes,
    fwd_gates,
    bwd_grads,
    bwd_routes,
    bwd_gates,
    saved_gate,
    saved_up,
    w_gate,
    w_up,
    w_down,
):
    tokens, grads = fwd_tokens[0], bwd_grads[0]
    width, inner = tokens.shape[1], w_gate.shape[3]
    quarter = width // 4
    any_, vmem = pl.BlockSpec(memory_space=pl.ANY), pl.BlockSpec(memory_space=pltpu.VMEM)

    def buf(*shape):
        return pltpu.VMEM(shape, BF16)

    scratch = (
        [buf(ROWS, width)] * 8
        + [buf(2 * ROWS, width)] * 2
        + [buf(2, 2, 4 * TAIL, quarter)] * 4
        + [buf(2, 2, TOK, width // 2)] * 2
        + [buf(2, 2, TOK, width)] * 2
        + [buf(2, TOK, width)]
        + [buf(2, 2, 4, 16, LANES)]
        + [buf(2, 4, 16, LANES)] * 3
        + [pltpu.VMEM((8, LANES), F32), pltpu.VMEM((8, TOK * 8), F32)]
        + [buf(ROWS, 2 * inner)] * 4
        + [buf(MAIN, 2 * inner), buf(2 * ROWS, 2 * inner)]
        + [buf(2, 4 * TAIL, inner // 2)] * 2
        + [buf(4 * TAIL, inner // 2)]
        + [buf(2, 4 * TAIL, inner // 2)] * 2
        + [buf(2 * ROWS, 2 * inner), buf(ROWS, TOK * 8), buf(2, 2, MAIN, ROWS), pltpu.VMEM((ROWS, LANES), F32)]
        + [buf(2, width, 256), buf(2, 256, width)]
        + [pltpu.SemaphoreType.DMA((N_SEMS,)), pltpu.SemaphoreType.DMA((N_SEMS,))]
        + [pltpu.SemaphoreType.DMA((N_LOCAL,)), pltpu.SemaphoreType.DMA((4, 2))]
    )
    out = jax.ShapeDtypeStruct(tokens.shape, BF16)
    rows = 2 * ROWS
    fo, fp, bo, bp = pl.pallas_call(
        kernel,
        out_shape=(out,) * 4,
        in_specs=[any_] * 7 + [vmem] * 6,
        out_specs=(any_,) * 4,
        scratch_shapes=scratch,
        compiler_params=pltpu.CompilerParams(
            collective_id=1, has_side_effects=True, vmem_limit_bytes=62 * 1024 * 1024
        ),
        cost_estimate=pl.CostEstimate(
            flops=12 * rows * width * inner, bytes_accessed=12 * width * inner, transcendentals=2 * rows * inner
        ),
    )(
        tokens,
        grads,
        saved_gate[0].reshape(-1, inner),
        saved_up[0].reshape(-1, inner),
        w_gate[0, 0],
        w_up[0, 0],
        w_down[0, 0],
        fwd_routes[0].T,
        fwd_gates[0].T,
        bwd_routes[0].T,
        bwd_gates[0].T,
        jnp.asarray(fold_matrix(), BF16),
        jnp.asarray(swap_matrix(), BF16),
    )
    next_inputs = (fo.astype(F32) + fp.astype(F32)).astype(BF16)
    prev_grads = (bo.astype(F32) + bp.astype(F32)).astype(BF16)
    return (next_inputs[None], prev_grads[None])


def solution(mesh):
    return jax.shard_map(
        body,
        mesh=mesh,
        in_specs=(P("section", "expert", None),) * 6 + (P("section", "expert", None, None),) * 5,
        out_specs=(P("section", "expert", None), P("section", "expert", None)),
        check_vma=False,
    )
```

time: 320 us -> 262 us (0.82)
  Pallas kernels: 302 us -> 255 us
  local copies, waits for them, and re-layouts: 4.73 us -> 0 us
    pallas_call x1, Pallas kernels: 302 us -> 255 us  [body(): pl.pallas_call(kernel, out_shape=(out,) * 4, in_specs=[any_] * 7 + [vmem]...]
    unnamed x2 -> x0, local copies, waits for them, and re-layouts: 3.81 us -> none
where the time goes in v2:
time: 262 us; the launch traced here: 259 us
  Pallas kernels  255 us (97%)
  other arithmetic  2.84 us (1%)
    pallas_call x1, Pallas kernels, body(): pl.pallas_call(kernel, out_shape=(out,) * 4, in_specs=[any_] * 7 + [vmem]...  255 us

profile of v2, /device:TPU:10, one launch (start us, length us, event | category | flops | bytes accessed | tf_op | source)
XLA Modules:
  0.0 258.6 jit_solution(11668899878737987653)
XLA Ops:
  0.6 255.1 %shard_map.140 = (bf16[80,3584]{1,0:T(8,128)(2,1)}, bf16[80,3584]{1,0:T(8,128)(2,1)}, bf16[80,3584]{1,0:T(8,128)(2,1)}, bf16[80,3584]{1,0:T(8,128)(2,1)}) custom-call(bf16[80,3584]{1,0:T(8,128)(2,1)} %bitcast.28, bf16[80,3584]{1,0:T(8,128)(2,1)} %bitcast.29, bf16[640,1024]{1,0:T(8,128)(2,1)} %bitcast.26, bf16[640,1024]{1,0:T(8,128)(2,1)} %bitcast.27, ...), custom_call_target="tpu_custom_call" | custom-call | flops 29595009024 | bytes 44040192 | tf_op jit(solution)/shard_map/pallas_call | solution.py:668
  255.8 2.8 %fusion = (bf16[1,80,3584]{2,1,0:T(8,128)(2,1)}, bf16[1,80,3584]{2,1,0:T(8,128)(2,1)}) fusion(bf16[80,3584]{1,0:T(8,128)(2,1)} %get-tuple-element.7, bf16[80,3584]{1,0:T(8,128)(2,1)} %get-tuple-element.6, bf16[80,3584]{1,0:T(8,128)(2,1)} %get-tuple-element.9, bf16[80,3584]{1,0:T(8,128)(2,1)} %get-tuple-element.8), kind=kLoop, calls=%fused_computation.2 | loop fusion | flops 2293760 | bytes 3440640 | tf_op jit(solution)/shard_map/broadcast_in_dim | solution.py:697

commit v3 on v2

--- a/solution.py
+++ b/solution.py
@@ -21,7 +21,7 @@
 ROWS = RING * GROUP
 TAIL = ROWS - MAIN
 LANES = 128
-N_SEMS = 176
+N_SEMS = 192
 N_LOCAL = 24
 
 
@@ -79,7 +79,7 @@
     meta, mo, mz, mp, turn, spos,
     spk_o, spk_p, sg_o, sg_p, sz, sx,
     spe, sge, sze, s2e, sxe,
-    hb, oh, qm, gc, wa, wd_t,
+    hb, oh, ix, close, qm, gc, wa, wd_t,
     send, recv, local, wsem,
 ):
     e = lax.axis_index("expert")
@@ -247,6 +247,10 @@
             dst[row0 : row0 + TAIL, col0 + c * w4 : col0 + (c + 1) * w4] = a[c * TAIL : (c + 1) * TAIL, :]
 
     def exchange(axis, src, src_off, src_extra, dst, dst_off, dst_extra, cols=slice(None)):
+        cps, own_copy = exchange_main(axis, src, src_off, dst, dst_off, cols)
+        return cps + exchange_extra(axis, src_extra, dst_extra), own_copy
+
+    def exchange_main(axis, src, src_off, dst, dst_off, cols=slice(None)):
         m = me[axis]
         cps = []
         for k in (2, 1, 3):
@@ -255,12 +259,19 @@
                 src.at[pl.ds(pl.multiple_of(src_off + c * TOK, 16), TOK), cols],
                 dst.at[pl.ds(pl.multiple_of(dst_off + m * TOK, 16), TOK), cols],
                 at(axis, c)))
-            cps.append(remote(src_extra.at[aligned(c, TAIL), :], dst_extra.at[aligned(m, TAIL), :], at(axis, c)))
-        own = here(
+        own_copy = here(
             src.at[pl.ds(pl.multiple_of(src_off + m * TOK, 16), TOK), cols],
             dst.at[pl.ds(pl.multiple_of(dst_off + m * TOK, 16), TOK), cols])
+        return cps, own_copy
+
+    def exchange_extra(axis, src_extra, dst_extra):
+        m = me[axis]
+        cps = []
+        for k in (2, 1, 3):
+            c = lax.rem(m + k, RING)
+            cps.append(remote(src_extra.at[aligned(c, TAIL), :], dst_extra.at[aligned(m, TAIL), :], at(axis, c)))
         dst_extra[aligned(m, TAIL), :] = src_extra[aligned(m, TAIL), :]
-        return cps, own
+        return cps
 
     def slot_of(ref, c, cols=None):
         rows = pl.ds(pl.multiple_of(c * TOK, 16), TOK)
@@ -268,21 +279,22 @@
 
     LO, HI = pl.ds(0, half), pl.ds(half, half)
 
-    def gather_begin(axis, ref):
+    def gather_begin(axis, ref, cols):
         m = me[axis]
-        return [remote(slot_of(ref, m), slot_of(ref, m), peer(axis, 1)),
-                remote(slot_of(ref, m), slot_of(ref, m), peer(axis, 3))]
-
-    def gather_relay(axis, ref, first):
+        return [remote(slot_of(ref, m, cols), slot_of(ref, m, cols), peer(axis, k))
+                for k in ((1, 3) if cols is LO else (3, 1))]
+
+    def gather_relay(axis, ref, low, high):
         m = me[axis]
         before, after = lax.rem(m + 3, RING), lax.rem(m + 1, RING)
-        first[0].wait_recv()
+        low[0].wait_recv()
         a = remote(slot_of(ref, before, LO), slot_of(ref, before, LO), peer(axis, 1))
-        first[1].wait_recv()
+        high[0].wait_recv()
         b = remote(slot_of(ref, after, HI), slot_of(ref, after, HI), peer(axis, 3))
-        return [a, b]
-
-    def pack(f, g):
+        return [a, b, low[1], high[1]]
+
+    def pack_index(f, g, notes):
+        wait_recv(notes)
         wide = lax.broadcasted_iota(jnp.int32, (TOK, LANES), 0).astype(F32)
         tail = lax.broadcasted_iota(jnp.int32, (TAIL, LANES), 0)
         tail_place = (TOK + lax.rem(tail, EXTRA)).astype(F32)
@@ -310,16 +322,17 @@
             tail_gate += jnp.sum(jnp.where(hit, weight, 0.0), axis=1, keepdims=True)
         if f == B:
             for t in range(RING):
-                gc[t * TOK : (t + 1) * TOK, :] = jnp.broadcast_to(gate[t], (TOK, LANES))
-            gc[MAIN:ROWS, :] = jnp.broadcast_to(tail_gate, (TAIL, LANES))
-
+                gc[g, t * TOK : (t + 1) * TOK, :] = jnp.broadcast_to(gate[t], (TOK, LANES))
+            gc[g, MAIN:ROWS, :] = jnp.broadcast_to(tail_gate, (TAIL, LANES))
+
+        ix[f, g] = dot(oh[:, 0 : RING * LANES], close[...]).astype(BF16)
+
+    def pack_rows(f, g):
         def cols_step(j, carry):
             cols = aligned(j, 512)
-            acc = dot(oh[:, 0:TOK], G[f][g][0:TOK, cols])
-            for q in range(1, RING):
-                acc = acc + dot(oh[:, q * LANES : q * LANES + TOK], G[f][g][q * TOK : (q + 1) * TOK, cols])
+            acc = dot(ix[f, g], G[f][g][0:MAIN, cols])
             if f == B:
-                acc = acc * gc[:, 0:1]
+                acc = acc * gc[g, :, 0:1]
             PK[f][g][:, cols] = acc.astype(BF16)
             return carry
 
@@ -404,14 +417,15 @@
     everyone += [peer(a, k) for a in ("y", "x") for k in (1, 2, 3)]
     for device in everyone:
         pl.semaphore_signal(barrier, inc=1, device_id=device, device_id_type=MESH)
+    c = lax.broadcasted_iota(jnp.int32, close.shape, 0)
+    j = lax.broadcasted_iota(jnp.int32, close.shape, 1)
+    same = jnp.logical_and(c // LANES == j // TOK, lax.rem(c, LANES) == lax.rem(j, TOK))
+    close[...] = jnp.where(same, 1.0, 0.0).astype(BF16)
     pl.semaphore_wait(barrier, len(everyone))
 
-    def gather_first(f):
-        own[f].wait()
-        return gather_begin(AG_AXIS[f][O], G[f][O])
-
-    def partner_send(f):
-        return remote(slot_of(G[f][O], me[AG_AXIS[f][O]]), slot_of(G[f][Q], me[AG_AXIS[f][Q]]), partner)
+    def partner_send(f, cols):
+        return remote(
+            slot_of(G[f][O], me[AG_AXIS[f][O]], cols), slot_of(G[f][Q], me[AG_AXIS[f][Q]], cols), partner)
 
     def notes_begin(f):
         axis = AG_AXIS[f][O]
@@ -423,25 +437,29 @@
         mo[f, m] = meta[f, O, m]
         return notes
 
-    def partner_begin(f, to_z, notes):
+    def partner_notes(f, notes):
         axis = AG_AXIS[f][Q]
         m = me[axis]
-        to_z.wait_recv()
-        first = gather_begin(axis, G[f][Q])
         notes[0].wait_recv()
         more = []
         for k in (1, 2, 3):
             c = lax.rem(m + k, RING)
             more.append(remote(mz.at[f, c], mp.at[f, m], at(axis, c)))
         mp[f, m] = mz[f, m]
-        return first, more
-
-    def packed(f, g, sent, relays, notes):
-        wait_recv(notes)
+        return more
+
+    def partner_begin(f, to_z, cols):
+        to_z.wait_recv()
+        return gather_begin(AG_AXIS[f][Q], G[f][Q], cols)
+
+    def packed(f, g, relays):
         wait_recv(relays)
-        wait_send(sent + relays)
-        pack(f, g)
-        return exchange(UNI_AXIS[f][g], PK[f][g], 0, es.at[f, g], X[f], g * ROWS, er.at[f, g])
+        pack_rows(f, g)
+        return exchange_main(UNI_AXIS[f][g], PK[f][g], 0, X[f], g * ROWS)
+
+    def packed_extra(f, g, sent, relays):
+        wait_send(sent + relays[0:2])
+        return exchange_extra(UNI_AXIS[f][g], es.at[f, g], er.at[f, g])
 
     def saved_pack(g, dst):
         index = (lax.broadcasted_iota(jnp.int32, (ROWS, TOK * 8), 0) + g * ROWS).astype(F32)
@@ -455,32 +473,50 @@
         lax.fori_loop(0, 2 * inner // 512, cols_step, 0)
         fold_out(dst, MAIN, spe.at[g])
 
-    o_f = gather_first(F)
-    z_f = partner_send(F)
-    o_b = gather_first(B)
+    own[F].wait()
+    of_l = gather_begin("y", g_fo, LO)
+    zf_l = partner_send(F, LO)
+    of_h = gather_begin("y", g_fo, HI)
+    own[B].wait()
+    ob_l = gather_begin("x", g_bo, LO)
+    zb_l = partner_send(B, LO)
+    ob_h = gather_begin("x", g_bo, HI)
     places(F, routes_f, gates_f)
     n_f = notes_begin(F)
     places(B, routes_b, gates_b)
     n_b = notes_begin(B)
+    ro_f = gather_relay("y", g_fo, of_l, of_h)
+    ro_b = gather_relay("x", g_bo, ob_l, ob_h)
+    pf_l = partner_begin(F, zf_l, LO)
+    pb_l = partner_begin(B, zb_l, LO)
+    zf_h = partner_send(F, HI)
+    zb_h = partner_send(B, HI)
+    pack_index(F, O, n_f[1:])
+    pack_index(B, O, n_b[1:])
     for cp in saved_in:
         cp.wait()
     saved_pack(Q, spk_p)
-    ro_f = gather_relay("y", g_fo, o_f)
-    ro_b = gather_relay("x", g_bo, o_b)
-    p_f, np_f = partner_begin(F, z_f, n_f)
-    z_b = partner_send(B)
-    uo_f, lo_f = packed(F, O, [z_f] + o_f, ro_f, n_f[1:])
-    uo_b, lo_b = packed(B, O, [z_b] + o_b, ro_b, n_b[1:])
-    p_b, np_b = partner_begin(B, z_b, n_b)
+    uo_f, lo_f = packed(F, O, ro_f)
+    uo_b, lo_b = packed(B, O, ro_b)
+    pf_h = partner_begin(F, zf_h, HI)
+    pb_h = partner_begin(B, zb_h, HI)
     s1_z = [remote(spk_p.at[0:MAIN, :], sz, partner), remote(spe.at[1], sze, partner)]
-    rp_f = gather_relay("x", g_fp, p_f)
+    np_f = partner_notes(F, n_f)
+    np_b = partner_notes(B, n_b)
+    uo_f += packed_extra(F, O, [zf_l, zf_h] + of_l + of_h, ro_f)
+    uo_b += packed_extra(B, O, [zb_l, zb_h] + ob_l + ob_h, ro_b)
+    rp_f = gather_relay("x", g_fp, pf_l, pf_h)
+    rp_b = gather_relay("y", g_bp, pb_l, pb_h)
+    pack_index(F, Q, np_f)
+    pack_index(B, Q, np_b)
     saved_pack(O, spk_o)
+    up_f, lp_f = packed(F, Q, rp_f)
+    up_f += packed_extra(F, Q, pf_l + pf_h, rp_f)
     s1_o, sl_o = exchange("x", spk_o, 0, spe.at[0], sg_o, 0, sge.at[0])
+    up_b, lp_b = packed(B, Q, rp_b)
+    up_b += packed_extra(B, Q, pb_l + pb_h, rp_b)
     weights(F, O)
-    up_f, lp_f = packed(F, Q, p_f, rp_f, np_f)
-    rp_b = gather_relay("y", g_bp, p_b)
     weights(F, Q)
-    up_b, lp_b = packed(B, Q, p_b, rp_b, np_b)
     wait_recv(s1_z)
     s1_p, sl_p = exchange("y", sz, 0, sze, sg_p, 0, sge.at[1])
 
@@ -499,7 +535,6 @@
         fold_out(out, MAIN, s2e.at[g])
         return exchange(UNI_AXIS[B][g], out, 0, s2e.at[g], sx, g * ROWS, sxe.at[g])
 
-    s2_o, sm_o = saved_second(O, s1_o, sl_o, s1_o, sg_o, spk_o)
     weights(B, O)
     weights(B, Q)
 
@@ -518,6 +553,7 @@
 
     stream(inner // LANES, wa_pair, fwd_hidden)
     begin(wa_down)
+    s2_o, sm_o = saved_second(O, s1_o, sl_o, s1_o, sg_o, spk_o)
     s2_p, sm_p = saved_second(Q, s1_p, sl_p, s1_z, sg_p, spk_p)
 
     def fwd_down(j, slot):
@@ -658,7 +694,8 @@
         + [buf(2, 4 * TAIL, inner // 2)] * 2
         + [buf(4 * TAIL, inner // 2)]
         + [buf(2, 4 * TAIL, inner // 2)] * 2
-        + [buf(2 * ROWS, 2 * inner), buf(ROWS, TOK * 8), buf(2, 2, MAIN, ROWS), pltpu.VMEM((ROWS, LANES), F32)]
+        + [buf(2 * ROWS, 2 * inner), buf(ROWS, TOK * 8), buf(2, 2, ROWS, MAIN), buf(RING * LANES, MAIN), buf(2, 2, MAIN, ROWS)]
+        + [pltpu.VMEM((2, ROWS, LANES), F32)]
         + [buf(2, width, 256), buf(2, 256, width)]
         + [pltpu.SemaphoreType.DMA((N_SEMS,)), pltpu.SemaphoreType.DMA((N_SEMS,))]
         + [pltpu.SemaphoreType.DMA((N_LOCAL,)), pltpu.SemaphoreType.DMA((4, 2))]

time: 262 us -> 243 us (0.927)
  Pallas kernels: 255 us -> 238 us
    pallas_call x1, Pallas kernels: 255 us -> 238 us  [body(): pl.pallas_call(kernel, out_shape=(out,) * 4, in_specs=[any_] * 7 + [vmem]...]
where the time goes in v3:
time: 243 us; the launch traced here: 241 us
  Pallas kernels  238 us (98%)
  other arithmetic  2.84 us (1%)
    pallas_call x1, Pallas kernels, body(): pl.pallas_call(kernel, out_shape=(out,) * 4, in_specs=[any_] * 7 + [vmem]...  238 us

profile of v3, /device:TPU:10, one launch (start us, length us, event | category | flops | bytes accessed | tf_op | source)
XLA Modules:
  0.0 241.4 jit_solution(3194409660855088361)
XLA Ops:
  0.6 237.9 %shard_map.140 = (bf16[80,3584]{1,0:T(8,128)(2,1)}, bf16[80,3584]{1,0:T(8,128)(2,1)}, bf16[80,3584]{1,0:T(8,128)(2,1)}, bf16[80,3584]{1,0:T(8,128)(2,1)}) custom-call(bf16[80,3584]{1,0:T(8,128)(2,1)} %bitcast.28, bf16[80,3584]{1,0:T(8,128)(2,1)} %bitcast.29, bf16[640,1024]{1,0:T(8,128)(2,1)} %bitcast.26, bf16[640,1024]{1,0:T(8,128)(2,1)} %bitcast.27, ...), custom_call_target="tpu_custom_call" | custom-call | flops 29595009024 | bytes 44040192 | tf_op jit(solution)/shard_map/pallas_call | solution.py:705
  238.5 2.8 %fusion = (bf16[1,80,3584]{2,1,0:T(8,128)(2,1)}, bf16[1,80,3584]{2,1,0:T(8,128)(2,1)}) fusion(bf16[80,3584]{1,0:T(8,128)(2,1)} %get-tuple-element.7, bf16[80,3584]{1,0:T(8,128)(2,1)} %get-tuple-element.6, bf16[80,3584]{1,0:T(8,128)(2,1)} %get-tuple-element.9, bf16[80,3584]{1,0:T(8,128)(2,1)} %get-tuple-element.8), kind=kLoop, calls=%fused_computation.2 | loop fusion | flops 2293760 | bytes 3440640 | tf_op jit(solution)/shard_map/broadcast_in_dim | solution.py:734

commit v4 on v3

--- a/solution.py
+++ b/solution.py
@@ -636,17 +636,17 @@
 
     stream(tiles, wd_pair, bwd_down, 0, cut)
     back_b0 = give_back(B, 0)
-    f0 = note(sums_begin(F, 0, back_f0, uo_f + up_f))
     stream(tiles, wd_pair, bwd_down, cut, tiles)
     back_b1 = give_back(B, 1)
+    f0 = note(sums_begin(F, 0, back_f0, uo_f + up_f))
     f1 = note(sums_begin(F, 1, back_f1, []))
     f0 = note(sums_relay(F, 0, f0))
+    b0 = note(sums_begin(B, 0, back_b0, uo_b + up_b))
     f1 = note(sums_relay(F, 1, f1))
     last += sums_end(F, 0, f0)
-    b0 = note(sums_begin(B, 0, back_b0, uo_b + up_b))
-    last += sums_end(F, 1, f1)
     b0 = note(sums_relay(B, 0, b0))
     b1 = note(sums_begin(B, 1, back_b1, []))
+    last += sums_end(F, 1, f1)
     last += sums_end(B, 0, b0)
     b1 = note(sums_relay(B, 1, b1))
     last += sums_end(B, 1, b1)

time: 243 us -> 242 us (level)
  Pallas kernels: 238 us -> 235 us
    pallas_call x1, Pallas kernels: 238 us -> 235 us  [body(): pl.pallas_call(kernel, out_shape=(out,) * 4, in_specs=[any_] * 7 + [vmem]...]
where the time goes in v4:
time: 242 us; the launch traced here: 238 us
  Pallas kernels  235 us (97%)
  other arithmetic  2.84 us (1%)
    pallas_call x1, Pallas kernels, body(): pl.pallas_call(kernel, out_shape=(out,) * 4, in_specs=[any_] * 7 + [vmem]...  235 us

profile of v4, /device:TPU:10, one launch (start us, length us, event | category | flops | bytes accessed | tf_op | source)
XLA Modules:
  0.0 238.4 jit_solution(16890900862846978165)
XLA Ops:
  0.6 234.9 %shard_map.140 = (bf16[80,3584]{1,0:T(8,128)(2,1)}, bf16[80,3584]{1,0:T(8,128)(2,1)}, bf16[80,3584]{1,0:T(8,128)(2,1)}, bf16[80,3584]{1,0:T(8,128)(2,1)}) custom-call(bf16[80,3584]{1,0:T(8,128)(2,1)} %bitcast.28, bf16[80,3584]{1,0:T(8,128)(2,1)} %bitcast.29, bf16[640,1024]{1,0:T(8,128)(2,1)} %bitcast.26, bf16[640,1024]{1,0:T(8,128)(2,1)} %bitcast.27, ...), custom_call_target="tpu_custom_call" | custom-call | flops 29595009024 | bytes 44040192 | tf_op jit(solution)/shard_map/pallas_call | solution.py:705
  235.6 2.8 %fusion = (bf16[1,80,3584]{2,1,0:T(8,128)(2,1)}, bf16[1,80,3584]{2,1,0:T(8,128)(2,1)}) fusion(bf16[80,3584]{1,0:T(8,128)(2,1)} %get-tuple-element.7, bf16[80,3584]{1,0:T(8,128)(2,1)} %get-tuple-element.6, bf16[80,3584]{1,0:T(8,128)(2,1)} %get-tuple-element.9, bf16[80,3584]{1,0:T(8,128)(2,1)} %get-tuple-element.8), kind=kLoop, calls=%fused_computation.2 | loop fusion | flops 2293760 | bytes 3440640 | tf_op jit(solution)/shard_map/broadcast_in_dim | solution.py:734

commit v5 on v4

--- a/solution.py
+++ b/solution.py
@@ -21,7 +21,7 @@
 ROWS = RING * GROUP
 TAIL = ROWS - MAIN
 LANES = 128
-N_SEMS = 192
+N_SEMS = 208
 N_LOCAL = 24
 
 
@@ -371,16 +371,22 @@
         col0, size = CHUNKS[h]
         return (pl.ds(col0, size // 2), pl.ds(col0 + size // 2, size // 2)), pl.ds(col0 // 2, size // 2), pl.ds(col0, size)
 
+    direct = {}
+
     def scatter_begin(f, g, h):
         axis, ref = AG_AXIS[f][g], PK[f][g]
         (lo, hi), short, _ = parts(h)
         far = lax.rem(me[axis] + 2, RING)
-        return [remote(slot_of(ref, far, lo), ra.at[f, g, :, short], peer(axis, 1)),
-                remote(slot_of(ref, far, hi), rb.at[f, g, :, short], peer(axis, 3))]
+        first = [remote(slot_of(ref, far, lo), ra.at[f, g, :, short], peer(axis, 1)),
+                 remote(slot_of(ref, far, hi), rb.at[f, g, :, short], peer(axis, 3))]
+        direct[f, g, h] = [
+            remote(slot_of(ref, lax.rem(me[axis] + k, RING), cols), dst.at[f, g, :, cols], peer(axis, k))
+            for k, cols, dst in ((1, hi, rc), (3, lo, rd))]
+        return first + direct[f, g, h]
 
     def scatter_relay(f, g, h, first):
         axis, ref = AG_AXIS[f][g], PK[f][g]
-        ends, short, whole = parts(h)
+        ends, short, _ = parts(h)
         m = me[axis]
         cps = []
         for i, (k, got, dst) in enumerate(((1, ra, rc), (3, rb, rd))):
@@ -388,13 +394,13 @@
             c = lax.rem(m + k, RING)
             rows = pl.ds(pl.multiple_of(c * TOK, 16), TOK)
             ref[rows, ends[i]] = (ref[rows, ends[i]].astype(F32) + got[f, g, :, short].astype(F32)).astype(BF16)
-            cps.append(remote(slot_of(ref, c, whole), dst.at[f, g, :, whole], peer(axis, k)))
+            cps.append(remote(slot_of(ref, c, ends[i]), dst.at[f, g, :, ends[i]], peer(axis, k)))
         return cps
 
     def scatter_end(f, g, h, cps, out, device):
         axis, ref = AG_AXIS[f][g], PK[f][g]
         col0, size = CHUNKS[h]
-        wait_recv(cps)
+        wait_recv(cps + direct[f, g, h])
         rows = pl.ds(pl.multiple_of(me[axis] * TOK, 16), TOK)
 
         def cols_step(j, carry):

time: 242 us -> 243 us (level)
  no operation moved by 1% of the time
where the time goes in v5:
time: 243 us; the launch traced here: 240 us
  Pallas kernels  237 us (98%)
  other arithmetic  2.84 us (1%)
    pallas_call x1, Pallas kernels, body(): pl.pallas_call(kernel, out_shape=(out,) * 4, in_specs=[any_] * 7 + [vmem]...  237 us

profile of v5, /device:TPU:10, one launch (start us, length us, event | category | flops | bytes accessed | tf_op | source)
XLA Modules:
  0.0 240.5 jit_solution(8645553620535485536)
XLA Ops:
  0.6 237.0 %shard_map.140 = (bf16[80,3584]{1,0:T(8,128)(2,1)}, bf16[80,3584]{1,0:T(8,128)(2,1)}, bf16[80,3584]{1,0:T(8,128)(2,1)}, bf16[80,3584]{1,0:T(8,128)(2,1)}) custom-call(bf16[80,3584]{1,0:T(8,128)(2,1)} %bitcast.28, bf16[80,3584]{1,0:T(8,128)(2,1)} %bitcast.29, bf16[640,1024]{1,0:T(8,128)(2,1)} %bitcast.26, bf16[640,1024]{1,0:T(8,128)(2,1)} %bitcast.27, ...), custom_call_target="tpu_custom_call" | custom-call | flops 29595009024 | bytes 44040192 | tf_op jit(solution)/shard_map/pallas_call | solution.py:711
  237.7 2.8 %fusion = (bf16[1,80,3584]{2,1,0:T(8,128)(2,1)}, bf16[1,80,3584]{2,1,0:T(8,128)(2,1)}) fusion(bf16[80,3584]{1,0:T(8,128)(2,1)} %get-tuple-element.7, bf16[80,3584]{1,0:T(8,128)(2,1)} %get-tuple-element.6, bf16[80,3584]{1,0:T(8,128)(2,1)} %get-tuple-element.9, bf16[80,3584]{1,0:T(8,128)(2,1)} %get-tuple-element.8), kind=kLoop, calls=%fused_computation.2 | loop fusion | flops 2293760 | bytes 3440640 | tf_op jit(solution)/shard_map/broadcast_in_dim | solution.py:740
